TPU v7x, 512 devices: a whole 4x8x8 slice. The times are simulated.
512 devices in a mesh: blk: 128 (over y, z, x_lo), rep: 4 (over x_hi, core).
Axes of the slice: x: 4 (x_hi: 2, x_lo: 2; x = x_hi * 2 + x_lo), y: 8, z: 8, core: 2. Of those that a mesh axis runs over, the one named last changes fastest.
Arguments:
- resident_keys: int32 [262144], P('blk'), may hold values from 0 to 4095
- moving_keys: int32 [1048576], P(('blk', 'rep')), may hold values from 0 to 4095
- payload: float32 [1048576, 128], P(('blk', 'rep')), may hold values from -6 to 6
Outputs:
- joined: float32 [262144, 128], P(('blk', 'rep'))
All inputs are finite; a program needn't handle non-finite values.
Results may differ from a plain program's by a relative error of at most 0.0003.
Values sent between devices are 32-bit elements; how exact they have to be, the bound alone decides.
No kernel may reach another device: no remote copies, remote signals or barrier semaphores. Data moves between devices by JAX's collectives and lax.ppermute only.
A program may use at most 64 MiB of HBM per device.

v0:
```python
import jax
import jax.numpy as jnp
from jax import lax
from jax.sharding import PartitionSpec as P

REACH = 2


def from_behind(block, axis, distance):
    devices = range(lax.axis_size(axis))
    route = [((i - distance) % len(devices), i) for i in devices]
    return lax.ppermute(block, axis, route)


def cut_along(array, dim, size):
    lengths = array.shape
    parts = array.reshape(*lengths[:dim], size, lengths[dim] // size, *lengths[dim + 1 :])
    return jnp.moveaxis(parts, dim, 0)


def summed_on_arrival(array, axis, dim):
    parts = cut_along(array, dim, lax.axis_size(axis))
    arrived = lax.all_to_all(parts, axis, split_axis=0, concat_axis=0, tiled=True)
    return arrived.sum(axis=0)


def match_rows(res_keys, mov_keys, mov_pay):
    count = res_keys.shape[0]
    block = min(512, count)
    grouped = res_keys.reshape(count // block, block)

    def one_block(keys_here):
        hot = (keys_here[:, None] == mov_keys[None, :]).astype(jnp.float32)
        return jnp.dot(
            hot, mov_pay, precision=lax.Precision.HIGHEST, preferred_element_type=jnp.float32
        )

    return lax.map(one_block, grouped).reshape(count, mov_pay.shape[1])


def local(resident_keys, moving_keys, payload):
    total = match_rows(resident_keys, moving_keys, payload)
    for distance in range(1, REACH + 1):
        upward = from_behind((moving_keys, payload), "blk", distance)
        total = total + match_rows(resident_keys, upward[0], upward[1])
        downward = from_behind((moving_keys, payload), "blk", -distance)
        total = total + match_rows(resident_keys, downward[0], downward[1])
    return summed_on_arrival(total, "rep", 0)


def solution(mesh):
    in_specs = (P("blk"), P(("blk", "rep")), P(("blk", "rep"), None))
    out_specs = P(("blk", "rep"), None)
    return jax.shard_map(local, mesh=mesh, in_specs=in_specs, out_specs=out_specs, check_vma=False)
```

profile of v0, /device:TPU:1, one launch (start us, length us, event | category | flops | bytes accessed | tf_op | source)
XLA Modules:
  0.0 146.1 jit_solution(14114420042434206292)
XLA Ops:
  0.0 4.1 %collective-permute-start.1 = (f32[2048,128]{1,0:T(8,128)}, f32[2048,128]{1,0:T(8,128)S(1)}, u32[]{:S(2)}, u32[]{:S(2)}) collective-permute-start(f32[2048,128]{1,0:T(8,128)} %param.15), channel_id=1, source_target_pairs={{508,0},{0,4},{4,8},{8,12},{12,16},{16,20},{20,24},{24,28},{28,32}... | collective-permute-start | bytes 3145736 | tf_op jit(solution)/shard_map/ppermute | solution.py:12
  4.1 13.3 %collective-permute-start.3 = (f32[2048,128]{1,0:T(8,128)}, f32[2048,128]{1,0:T(8,128)}, u32[]{:S(2)}, u32[]{:S(2)}) collective-permute-start(f32[2048,128]{1,0:T(8,128)} %param.15), channel_id=1, source_target_pairs={{4,0},{8,4},{12,8},{16,12},{20,16},{24,20},{28,24},{32,28},{36,32}... | collective-permute-start | bytes 3145736 | tf_op jit(solution)/shard_map/ppermute | solution.py:12
  19.3 7.6 %collective-permute-start.2 = (s32[2048]{0:T(1024)}, s32[2048]{0:T(1024)S(1)}, u32[]{:S(2)}, u32[]{:S(2)}) collective-permute-start(s32[2048]{0:T(1024)} %param.14), channel_id=1, source_target_pairs={{4,0},{8,4},{12,8},{16,12},{20,16},{24,20},{28,24},{32,28},{36,32}... | collective-permute-start | bytes 24584 | tf_op jit(solution)/shard_map/ppermute | solution.py:12
  29.6 12.9 %while.50 = (s32[]{:T(128)}, f32[4,512,128]{2,1,0:T(8,128)S(1)}, s32[4,512]{1,0:T(4,128)S(1)}, s32[2048]{0:T(1024)S(1)}, f32[2048,128]{1,0:T(8,128)}, /*index=5*/s32[]{:T(128)}) while((s32[]{:T(128)}, f32[4,512,128]{2,1,0:T(8,128)S(1)}, s32[4,512]{1,0:T(4,128)S(1)}, s32[2048]{0:T(1024)S(1)}, f32[2048,128]{1,0:T(8,128)}, ...), condition=%wide.region_1.2_spmd, body=%wide.region_0.1_spmd.sunk | while | flops 1611661312 | bytes 1325133 | solution.py:38
  29.7 3.2 %fusion.72 = f32[4,512,128]{2,1,0:T(8,128)S(1)} fusion(f32[4,512,128]{2,1,0:T(8,128)S(1)} %get-tuple-element.411, s32[]{:T(128)} %get-tuple-element.410, f32[2048,128]{1,0:T(8,128)} %get-tuple-element.420, s32[2048]{0:T(1024)S(1)} %get-tuple-element.419, s32[512]{0:T(512)S(1)} %bitcast.60), kind=kOutput, calls=%fused_computation.5.clone.1 | convolution fusion | flops 1611661312 | bytes 1320964 | tf_op jit(solution)/shard_map/while/body/eval_jaxpr/dot_general | solution.py:34
  32.9 3.2 %fusion.72 = f32[4,512,128]{2,1,0:T(8,128)S(1)} fusion(f32[4,512,128]{2,1,0:T(8,128)S(1)} %get-tuple-element.411, s32[]{:T(128)} %get-tuple-element.410, f32[2048,128]{1,0:T(8,128)} %get-tuple-element.420, s32[2048]{0:T(1024)S(1)} %get-tuple-element.419, s32[512]{0:T(512)S(1)} %bitcast.60), kind=kOutput, calls=%fused_computation.5.clone.1 | convolution fusion | flops 1611661312 | bytes 1320964 | tf_op jit(solution)/shard_map/while/body/eval_jaxpr/dot_general | solution.py:34
  36.1 3.2 %fusion.72 = f32[4,512,128]{2,1,0:T(8,128)S(1)} fusion(f32[4,512,128]{2,1,0:T(8,128)S(1)} %get-tuple-element.411, s32[]{:T(128)} %get-tuple-element.410, f32[2048,128]{1,0:T(8,128)} %get-tuple-element.420, s32[2048]{0:T(1024)S(1)} %get-tuple-element.419, s32[512]{0:T(512)S(1)} %bitcast.60), kind=kOutput, calls=%fused_computation.5.clone.1 | convolution fusion | flops 1611661312 | bytes 1320964 | tf_op jit(solution)/shard_map/while/body/eval_jaxpr/dot_general | solution.py:34
  39.4 3.2 %fusion.72 = f32[4,512,128]{2,1,0:T(8,128)S(1)} fusion(f32[4,512,128]{2,1,0:T(8,128)S(1)} %get-tuple-element.411, s32[]{:T(128)} %get-tuple-element.410, f32[2048,128]{1,0:T(8,128)} %get-tuple-element.420, s32[2048]{0:T(1024)S(1)} %get-tuple-element.419, s32[512]{0:T(512)S(1)} %bitcast.60), kind=kOutput, calls=%fused_computation.5.clone.1 | convolution fusion | flops 1611661312 | bytes 1320964 | tf_op jit(solution)/shard_map/while/body/eval_jaxpr/dot_general | solution.py:34
  42.6 2.5 %collective-permute-done = s32[2048]{0:T(1024)S(1)} collective-permute-done((s32[2048]{0:T(1024)}, s32[2048]{0:T(1024)S(1)}, u32[]{:S(2)}, u32[]{:S(2)}) %collective-permute-start) | collective-permute-done | bytes 8224 | tf_op jit(solution)/shard_map/ppermute | solution.py:12
  45.0 7.9 %collective-permute-start.4 = (s32[2048]{0:T(1024)S(1)}, s32[2048]{0:T(1024)S(1)}, u32[]{:S(2)}, u32[]{:S(2)}) collective-permute-start(s32[2048]{0:T(1024)S(1)} %get-tuple-element.447), channel_id=1, source_target_pairs={{504,0},{508,4},{0,8},{4,12},{8,16},{12,20},{16,24},{20,28},{24,32... | collective-permute-start | bytes 24584 | tf_op jit(solution)/shard_map/ppermute | solution.py:12
  52.9 11.5 %collective-permute-start.7 = (f32[2048,128]{1,0:T(8,128)}, f32[2048,128]{1,0:T(8,128)}, u32[]{:S(2)}, u32[]{:S(2)}) collective-permute-start(f32[2048,128]{1,0:T(8,128)} %param.15), channel_id=1, source_target_pairs={{8,0},{12,4},{16,8},{20,12},{24,16},{28,20},{32,24},{36,28},{40,32... | collective-permute-start | bytes 3145736 | tf_op jit(solution)/shard_map/ppermute | solution.py:12
  64.5 8.0 %while.51 = (s32[]{:T(128)}, f32[4,512,128]{2,1,0:T(8,128)S(1)}, s32[4,512]{1,0:T(4,128)S(1)}, s32[2048]{0:T(1024)S(1)}, f32[2048,128]{1,0:T(8,128)S(1)}, /*index=5*/s32[]{:T(128)}) while((s32[]{:T(128)}, f32[4,512,128]{2,1,0:T(8,128)S(1)}, s32[4,512]{1,0:T(4,128)S(1)}, s32[2048]{0:T(1024)S(1)}, f32[2048,128]{1,0:T(8,128)S(1)}, ...), condition=%wide.region_3.4_spmd, body=%wide.region_2.3_spmd.sunk | while | flops 1611661312 | bytes 1325133 | solution.py:38
  66.5 2.0 %fusion.75 = f32[4,512,128]{2,1,0:T(8,128)S(1)} fusion(f32[4,512,128]{2,1,0:T(8,128)S(1)} %get-tuple-element.429, s32[]{:T(128)} %get-tuple-element.428, f32[2048,128]{1,0:T(8,128)S(1)} %get-tuple-element.438, s32[2048]{0:T(1024)S(1)} %get-tuple-element.437, s32[512]{0:T(512)S(1)} %bitcast.61), kind=kOutput, calls=%fused_computation.12.clone.1 | convolution fusion | flops 1611661312 | bytes 1320964 | tf_op jit(solution)/shard_map/while/body/eval_jaxpr/dot_general | solution.py:34
  68.6 2.0 %fusion.75 = f32[4,512,128]{2,1,0:T(8,128)S(1)} fusion(f32[4,512,128]{2,1,0:T(8,128)S(1)} %get-tuple-element.429, s32[]{:T(128)} %get-tuple-element.428, f32[2048,128]{1,0:T(8,128)S(1)} %get-tuple-element.438, s32[2048]{0:T(1024)S(1)} %get-tuple-element.437, s32[512]{0:T(512)S(1)} %bitcast.61), kind=kOutput, calls=%fused_computation.12.clone.1 | convolution fusion | flops 1611661312 | bytes 1320964 | tf_op jit(solution)/shard_map/while/body/eval_jaxpr/dot_general | solution.py:34
  70.6 2.0 %fusion.75 = f32[4,512,128]{2,1,0:T(8,128)S(1)} fusion(f32[4,512,128]{2,1,0:T(8,128)S(1)} %get-tuple-element.429, s32[]{:T(128)} %get-tuple-element.428, f32[2048,128]{1,0:T(8,128)S(1)} %get-tuple-element.438, s32[2048]{0:T(1024)S(1)} %get-tuple-element.437, s32[512]{0:T(512)S(1)} %bitcast.61), kind=kOutput, calls=%fused_computation.12.clone.1 | convolution fusion | flops 1611661312 | bytes 1320964 | tf_op jit(solution)/shard_map/while/body/eval_jaxpr/dot_general | solution.py:34
  72.6 3.4 %collective-permute-start.6 = (s32[2048]{0:T(1024)S(1)}, s32[2048]{0:T(1024)S(1)}, u32[]{:S(2)}, u32[]{:S(2)}) collective-permute-start(s32[2048]{0:T(1024)S(1)} %get-tuple-element.447), channel_id=1, source_target_pairs={{8,0},{12,4},{16,8},{20,12},{24,16},{28,20},{32,24},{36,28},{40,32... | collective-permute-start | bytes 24584 | tf_op jit(solution)/shard_map/ppermute | solution.py:12
  76.0 12.9 %while.52 = (s32[]{:T(128)}, f32[4,512,128]{2,1,0:T(8,128)S(1)}, s32[4,512]{1,0:T(4,128)S(1)}, s32[2048]{0:T(1024)S(1)}, f32[2048,128]{1,0:T(8,128)}, /*index=5*/s32[]{:T(128)}) while((s32[]{:T(128)}, f32[4,512,128]{2,1,0:T(8,128)S(1)}, s32[4,512]{1,0:T(4,128)S(1)}, s32[2048]{0:T(1024)S(1)}, f32[2048,128]{1,0:T(8,128)}, ...), condition=%wide.region_5.6_spmd, body=%wide.region_4.5_spmd.sunk | while | flops 1611661312 | bytes 1325133 | solution.py:38
  76.1 3.2 %fusion.78 = f32[4,512,128]{2,1,0:T(8,128)S(1)} fusion(f32[4,512,128]{2,1,0:T(8,128)S(1)} %get-tuple-element.393, s32[]{:T(128)} %get-tuple-element.392, f32[2048,128]{1,0:T(8,128)} %get-tuple-element.402, s32[2048]{0:T(1024)S(1)} %get-tuple-element.401, s32[512]{0:T(512)S(1)} %bitcast.62), kind=kOutput, calls=%fused_computation.19.clone.1 | convolution fusion | flops 1611661312 | bytes 1320964 | tf_op jit(solution)/shard_map/while/body/eval_jaxpr/dot_general | solution.py:34
  79.3 3.2 %fusion.78 = f32[4,512,128]{2,1,0:T(8,128)S(1)} fusion(f32[4,512,128]{2,1,0:T(8,128)S(1)} %get-tuple-element.393, s32[]{:T(128)} %get-tuple-element.392, f32[2048,128]{1,0:T(8,128)} %get-tuple-element.402, s32[2048]{0:T(1024)S(1)} %get-tuple-element.401, s32[512]{0:T(512)S(1)} %bitcast.62), kind=kOutput, calls=%fused_computation.19.clone.1 | convolution fusion | flops 1611661312 | bytes 1320964 | tf_op jit(solution)/shard_map/while/body/eval_jaxpr/dot_general | solution.py:34
  82.5 3.2 %fusion.78 = f32[4,512,128]{2,1,0:T(8,128)S(1)} fusion(f32[4,512,128]{2,1,0:T(8,128)S(1)} %get-tuple-element.393, s32[]{:T(128)} %get-tuple-element.392, f32[2048,128]{1,0:T(8,128)} %get-tuple-element.402, s32[2048]{0:T(1024)S(1)} %get-tuple-element.401, s32[512]{0:T(512)S(1)} %bitcast.62), kind=kOutput, calls=%fused_computation.19.clone.1 | convolution fusion | flops 1611661312 | bytes 1320964 | tf_op jit(solution)/shard_map/while/body/eval_jaxpr/dot_general | solution.py:34
  85.8 3.2 %fusion.78 = f32[4,512,128]{2,1,0:T(8,128)S(1)} fusion(f32[4,512,128]{2,1,0:T(8,128)S(1)} %get-tuple-element.393, s32[]{:T(128)} %get-tuple-element.392, f32[2048,128]{1,0:T(8,128)} %get-tuple-element.402, s32[2048]{0:T(1024)S(1)} %get-tuple-element.401, s32[512]{0:T(512)S(1)} %bitcast.62), kind=kOutput, calls=%fused_computation.19.clone.1 | convolution fusion | flops 1611661312 | bytes 1320964 | tf_op jit(solution)/shard_map/while/body/eval_jaxpr/dot_general | solution.py:34
  90.1 15.6 %while.53 = (s32[]{:T(128)}, f32[4,512,128]{2,1,0:T(8,128)}, s32[4,512]{1,0:T(4,128)S(1)}, s32[2048]{0:T(1024)S(1)}, f32[2048,128]{1,0:T(8,128)}, /*index=5*/s32[]{:T(128)}) while((s32[]{:T(128)}, f32[4,512,128]{2,1,0:T(8,128)}, s32[4,512]{1,0:T(4,128)S(1)}, s32[2048]{0:T(1024)S(1)}, f32[2048,128]{1,0:T(8,128)}, /*index=5*/s32[]{:T(128)}) %tuple.87), condition=%wide.region_7.8_spmd, body=%wide.region_6.7_spmd.sunk | while | flops 1611661312 | bytes 1325641 | solution.py:38
  90.1 3.9 %fusion.81 = f32[4,512,128]{2,1,0:T(8,128)} fusion(f32[4,512,128]{2,1,0:T(8,128)} %get-tuple-element.375, s32[]{:T(128)} %get-tuple-element.374, f32[2048,128]{1,0:T(8,128)} %get-tuple-element.384, s32[2048]{0:T(1024)S(1)} %get-tuple-element.383, s32[512]{0:T(512)S(1)} %bitcast.63), kind=kOutput, calls=%fused_computation.26.clone.1 | convolution fusion | flops 1611661312 | bytes 1321472 | tf_op jit(solution)/shard_map/while/body/eval_jaxpr/dot_general | solution.py:34
  94.0 3.9 %fusion.81 = f32[4,512,128]{2,1,0:T(8,128)} fusion(f32[4,512,128]{2,1,0:T(8,128)} %get-tuple-element.375, s32[]{:T(128)} %get-tuple-element.374, f32[2048,128]{1,0:T(8,128)} %get-tuple-element.384, s32[2048]{0:T(1024)S(1)} %get-tuple-element.383, s32[512]{0:T(512)S(1)} %bitcast.63), kind=kOutput, calls=%fused_computation.26.clone.1 | convolution fusion | flops 1611661312 | bytes 1321472 | tf_op jit(solution)/shard_map/while/body/eval_jaxpr/dot_general | solution.py:34
  97.9 3.9 %fusion.81 = f32[4,512,128]{2,1,0:T(8,128)} fusion(f32[4,512,128]{2,1,0:T(8,128)} %get-tuple-element.375, s32[]{:T(128)} %get-tuple-element.374, f32[2048,128]{1,0:T(8,128)} %get-tuple-element.384, s32[2048]{0:T(1024)S(1)} %get-tuple-element.383, s32[512]{0:T(512)S(1)} %bitcast.63), kind=kOutput, calls=%fused_computation.26.clone.1 | convolution fusion | flops 1611661312 | bytes 1321472 | tf_op jit(solution)/shard_map/while/body/eval_jaxpr/dot_general | solution.py:34
  101.8 3.9 %fusion.81 = f32[4,512,128]{2,1,0:T(8,128)} fusion(f32[4,512,128]{2,1,0:T(8,128)} %get-tuple-element.375, s32[]{:T(128)} %get-tuple-element.374, f32[2048,128]{1,0:T(8,128)} %get-tuple-element.384, s32[2048]{0:T(1024)S(1)} %get-tuple-element.383, s32[512]{0:T(512)S(1)} %bitcast.63), kind=kOutput, calls=%fused_computation.26.clone.1 | convolution fusion | flops 1611661312 | bytes 1321472 | tf_op jit(solution)/shard_map/while/body/eval_jaxpr/dot_general | solution.py:34
  106.7 15.6 %while.54 = (s32[]{:T(128)}, f32[4,512,128]{2,1,0:T(8,128)}, s32[4,512]{1,0:T(4,128)S(1)}, s32[2048]{0:T(1024)S(1)}, f32[2048,128]{1,0:T(8,128)}, /*index=5*/s32[]{:T(128)}) while((s32[]{:T(128)}, f32[4,512,128]{2,1,0:T(8,128)}, s32[4,512]{1,0:T(4,128)S(1)}, s32[2048]{0:T(1024)S(1)}, f32[2048,128]{1,0:T(8,128)}, /*index=5*/s32[]{:T(128)}) %tuple.88), condition=%wide.region_9.10_spmd, body=%wide.region_8.9_spmd.sunk | while | flops 1611661312 | bytes 1325641 | solution.py:38
  106.7 3.9 %fusion.84 = f32[4,512,128]{2,1,0:T(8,128)} fusion(f32[4,512,128]{2,1,0:T(8,128)} %get-tuple-element.357, s32[]{:T(128)} %get-tuple-element.356, f32[2048,128]{1,0:T(8,128)} %get-tuple-element.366, s32[2048]{0:T(1024)S(1)} %get-tuple-element.365, s32[512]{0:T(512)S(1)} %bitcast.64), kind=kOutput, calls=%fused_computation.33.clone.1 | convolution fusion | flops 1611661312 | bytes 1321472 | tf_op jit(solution)/shard_map/while/body/eval_jaxpr/dot_general | solution.py:34
  110.6 3.9 %fusion.84 = f32[4,512,128]{2,1,0:T(8,128)} fusion(f32[4,512,128]{2,1,0:T(8,128)} %get-tuple-element.357, s32[]{:T(128)} %get-tuple-element.356, f32[2048,128]{1,0:T(8,128)} %get-tuple-element.366, s32[2048]{0:T(1024)S(1)} %get-tuple-element.365, s32[512]{0:T(512)S(1)} %bitcast.64), kind=kOutput, calls=%fused_computation.33.clone.1 | convolution fusion | flops 1611661312 | bytes 1321472 | tf_op jit(solution)/shard_map/while/body/eval_jaxpr/dot_general | solution.py:34
  114.5 3.9 %fusion.84 = f32[4,512,128]{2,1,0:T(8,128)} fusion(f32[4,512,128]{2,1,0:T(8,128)} %get-tuple-element.357, s32[]{:T(128)} %get-tuple-element.356, f32[2048,128]{1,0:T(8,128)} %get-tuple-element.366, s32[2048]{0:T(1024)S(1)} %get-tuple-element.365, s32[512]{0:T(512)S(1)} %bitcast.64), kind=kOutput, calls=%fused_computation.33.clone.1 | convolution fusion | flops 1611661312 | bytes 1321472 | tf_op jit(solution)/shard_map/while/body/eval_jaxpr/dot_general | solution.py:34
  118.4 3.9 %fusion.84 = f32[4,512,128]{2,1,0:T(8,128)} fusion(f32[4,512,128]{2,1,0:T(8,128)} %get-tuple-element.357, s32[]{:T(128)} %get-tuple-element.356, f32[2048,128]{1,0:T(8,128)} %get-tuple-element.366, s32[2048]{0:T(1024)S(1)} %get-tuple-element.365, s32[512]{0:T(512)S(1)} %bitcast.64), kind=kOutput, calls=%fused_computation.33.clone.1 | convolution fusion | flops 1611661312 | bytes 1321472 | tf_op jit(solution)/shard_map/while/body/eval_jaxpr/dot_general | solution.py:34
  124.2 21.1 %all_to_all.5 = f32[4,512,128]{2,1,0:T(8,128)S(1)} all-to-all(f32[4,512,128]{2,1,0:T(8,128)S(1)} %add_add_fusion), channel_id=1, replica_groups=mesh['blk'=128,'rep'=4] {'rep'}, dimensions={0} | all-to-all | bytes 2097152 | tf_op jit(solution)/shard_map/all_to_all | solution.py:23
  (40 shorter events, 11.7 us)
Async XLA Ops:
  0.0 29.6 %copy-start = (s32[2048]{0:T(1024)S(1)}, s32[2048]{0:T(1024)}, u32[]{:S(2)}) copy-start(s32[2048]{0:T(1024)} %param.14) | copy-start | bytes 24580
  0.0 52.9 %collective-permute-start.1 = (f32[2048,128]{1,0:T(8,128)}, f32[2048,128]{1,0:T(8,128)S(1)}, u32[]{:S(2)}, u32[]{:S(2)}) collective-permute-start(f32[2048,128]{1,0:T(8,128)} %param.15), channel_id=1, source_target_pairs={{508,0},{0,4},{4,8},{8,12},{12,16},{16,20},{20,24},{24,28},{28,32}... | collective-permute-start | bytes 3145736 | tf_op jit(solution)/shard_map/ppermute | solution.py:12
  4.1 71.9 %collective-permute-start.3 = (f32[2048,128]{1,0:T(8,128)}, f32[2048,128]{1,0:T(8,128)}, u32[]{:S(2)}, u32[]{:S(2)}) collective-permute-start(f32[2048,128]{1,0:T(8,128)} %param.15), channel_id=1, source_target_pairs={{4,0},{8,4},{12,8},{16,12},{20,16},{24,20},{28,24},{32,28},{36,32}... | collective-permute-start | bytes 3145736 | tf_op jit(solution)/shard_map/ppermute | solution.py:12
  17.4 27.6 %collective-permute-start = (s32[2048]{0:T(1024)}, s32[2048]{0:T(1024)S(1)}, u32[]{:S(2)}, u32[]{:S(2)}) collective-permute-start(s32[2048]{0:T(1024)} %param.14), channel_id=1, source_target_pairs={{508,0},{0,4},{4,8},{8,12},{12,16},{16,20},{20,24},{24,28},{28,32}... | collective-permute-start | bytes 24584 | tf_op jit(solution)/shard_map/ppermute | solution.py:12
  19.3 53.2 %collective-permute-start.2 = (s32[2048]{0:T(1024)}, s32[2048]{0:T(1024)S(1)}, u32[]{:S(2)}, u32[]{:S(2)}) collective-permute-start(s32[2048]{0:T(1024)} %param.14), channel_id=1, source_target_pairs={{4,0},{8,4},{12,8},{16,12},{20,16},{24,20},{28,24},{32,28},{36,32}... | collective-permute-start | bytes 24584 | tf_op jit(solution)/shard_map/ppermute | solution.py:12
  26.9 62.1 %collective-permute-start.5 = (f32[2048,128]{1,0:T(8,128)}, f32[2048,128]{1,0:T(8,128)}, u32[]{:S(2)}, u32[]{:S(2)}) collective-permute-start(f32[2048,128]{1,0:T(8,128)} %param.15), channel_id=1, source_target_pairs={{504,0},{508,4},{0,8},{4,12},{8,16},{12,20},{16,24},{20,28},{24,32... | collective-permute-start | bytes 3145736 | tf_op jit(solution)/shard_map/ppermute | solution.py:12
  45.0 44.0 %collective-permute-start.4 = (s32[2048]{0:T(1024)S(1)}, s32[2048]{0:T(1024)S(1)}, u32[]{:S(2)}, u32[]{:S(2)}) collective-permute-start(s32[2048]{0:T(1024)S(1)} %get-tuple-element.447), channel_id=1, source_target_pairs={{504,0},{508,4},{0,8},{4,12},{8,16},{12,20},{16,24},{20,28},{24,32... | collective-permute-start | bytes 24584 | tf_op jit(solution)/shard_map/ppermute | solution.py:12
  52.9 52.7 %collective-permute-start.7 = (f32[2048,128]{1,0:T(8,128)}, f32[2048,128]{1,0:T(8,128)}, u32[]{:S(2)}, u32[]{:S(2)}) collective-permute-start(f32[2048,128]{1,0:T(8,128)} %param.15), channel_id=1, source_target_pairs={{8,0},{12,4},{16,8},{20,12},{24,16},{28,20},{32,24},{36,28},{40,32... | collective-permute-start | bytes 3145736 | tf_op jit(solution)/shard_map/ppermute | solution.py:12
  72.6 33.1 %collective-permute-start.6 = (s32[2048]{0:T(1024)S(1)}, s32[2048]{0:T(1024)S(1)}, u32[]{:S(2)}, u32[]{:S(2)}) collective-permute-start(s32[2048]{0:T(1024)S(1)} %get-tuple-element.447), channel_id=1, source_target_pairs={{8,0},{12,4},{16,8},{20,12},{24,16},{28,20},{32,24},{36,28},{40,32... | collective-permute-start | bytes 24584 | tf_op jit(solution)/shard_map/ppermute | solution.py:12
where the time goes:
time: 147 us; the launch traced here: 146 us
  matrix products  64.7 us (44%)
  starting transfers between devices  51.5 us (35%)
  blocking collectives  21.1 us (14%)
  local copies, waits for them, and re-layouts  3.16 us (2%)
  other arithmetic  2.7 us (2%)
  waiting for transfers between devices  2.47 us (2%)
    dot_general x20, matrix products, one_block(): jnp.dot(hot, mov_pay, precision=lax.Precision.HIGHEST, preferred_element_...  64.7 us
    ppermute x8, starting transfers between devices, from_behind(): return lax.ppermute(block, axis, route)  51.5 us
    all_to_all x1, blocking collectives, summed_on_arrival(): lax.all_to_all(parts, axis, split_axis=0, concat_axis=0, tiled=True)  21.1 us
  transfers between devices with their start and end apart: 8, of which 1 were waited for; matrix products, arithmetic and copies ran while one was open for 35% of the time, Pallas kernels for 0%

commit v1 on v0

v1 whole, which is shorter than its diff:
```python
import functools

import jax
import jax.numpy as jnp
from jax import lax
from jax.experimental import pallas as pl
from jax.experimental.pallas import tpu as pltpu
from jax.sharding import PartitionSpec as P

AXES = ("blk", "rep")
LANES = 128
QUARTER = 512
S_DEV = 2048
KEY_ROWS = 16
MOVING_KEYS = S_DEV // KEY_ROWS
FETCHED_KEYS = MOVING_KEYS + 1
VMEM_LIMIT = 24 * 1024 * 1024
HEAVY = 10**12


def device(block, half, core, blocks):
    return (block % blocks) * 4 + half * 2 + core


def routes(blocks):
    near, far_light, far_heavy, far_heavy_other, fetch, swap, halves = [], [], [], [], [], [], []
    for block in range(blocks):
        low = block % 2
        light = block - 2 if low == 0 else block + 2
        heavy = block + 2 if low == 0 else block - 2
        for half in range(2):
            for core in range(2):
                here = device(block, half, core, blocks)
                x = (half * 2 + low + (1 if core == 0 else -1)) % 4
                near.append((here, device(block - low + x % 2, x // 2, core, blocks)))
                far_light.append((here, device(light, half, core, blocks)))
                far_heavy.append((here, device(heavy, half, core, blocks)))
                far_heavy_other.append((here, device(heavy, 1 - half, core, blocks)))
                fetch.append((device(light if core == 0 else heavy, half, core, blocks), here))
                swap.append((here, device(block, half, 1 - core, blocks)))
                halves.append((here, device(block, 1 - half, core, blocks)))
    return near, far_light, far_heavy, far_heavy_other, fetch, swap, halves


def join_kernel(n_keys, raw, n_add, rows, second_core, n_out, *refs):
    place, refs = refs[0], refs[1:]
    key_refs, refs = refs[:n_keys], refs[n_keys:]
    moving_keys, refs = refs[: len(raw)], refs[len(raw) :]
    moving, refs = refs[: len(raw)], refs[len(raw) :]
    adds, refs = refs[:n_add], refs[n_add:]
    outs, refs = refs[:n_out], refs[n_out:]
    parts, (keys,) = refs[:-1], refs[-1:]
    half, core = place[0], place[1]
    if n_keys == 1:
        keys[...] = key_refs[0][...].astype(jnp.float32)
    else:
        keys[...] = jnp.where(core == second_core, key_refs[0][...], key_refs[1][...])
    columns = []
    for which in rows:
        quarter = (half if which == 0 else 1 - half) * 2 + core
        for j in range(QUARTER // LANES):
            row = keys[pl.ds(quarter * (QUARTER // LANES) + j, 1), :]
            columns.append(jnp.broadcast_to(row, (LANES, LANES)).T)
    resident = jnp.concatenate(columns, axis=0)
    count = resident.shape[0]
    total = jnp.zeros((count, 2 * LANES), jnp.float32)
    parts = list(parts)
    weights = [parts.pop(0) if is_raw else ref for is_raw, ref in zip(raw, moving)]
    for is_raw, ref, split in zip(raw, moving, weights):
        if is_raw:
            value = ref[pl.ds(0, S_DEV), :]
            high = value.astype(jnp.bfloat16)
            split[:, pl.ds(0, LANES)] = high
            split[:, pl.ds(LANES, LANES)] = (value - high.astype(jnp.float32)).astype(jnp.bfloat16)
    for key_rows, split in zip(moving_keys, weights):
        for k in range(S_DEV // 256):
            pieces = []
            for c in range(2):
                mov = key_rows[pl.ds(2 * k + c, 1), :]
                same = resident == jnp.broadcast_to(mov, (count, LANES))
                pieces.append(jnp.where(same, 1.0, 0.0).astype(jnp.bfloat16))
            hot = jnp.concatenate(pieces, axis=1)
            total = total + jnp.dot(hot, split[pl.ds(256 * k, 256), :], preferred_element_type=jnp.float32)
    joined = total[:, :LANES] + total[:, LANES:]
    for extra in adds:
        joined = joined + extra[...]
    each = count // n_out
    for i, out in enumerate(outs):
        out[...] = joined[i * each : (i + 1) * each]


def join(name, place, keys, moving, adds, rows, second_core=0, n_out=1, weight=0):
    count = QUARTER * len(rows)
    whole = pl.BlockSpec(memory_space=pltpu.VMEM)

    def block(height, number):
        return pl.BlockSpec((height, LANES), lambda i: (number, 0))

    raw = tuple(parts is None for _, parts in moving)
    sums = jax.ShapeDtypeStruct((count // n_out, LANES), jnp.float32)
    split = jax.ShapeDtypeStruct((S_DEV, 2 * LANES), jnp.bfloat16)
    return pl.pallas_call(
        functools.partial(join_kernel, len(keys), raw, len(adds), rows, second_core, n_out),
        grid=(1,),
        out_shape=[sums] * n_out + [split] * sum(raw),
        in_specs=[pl.BlockSpec(memory_space=pltpu.SMEM)]
        + [block(KEY_ROWS, number) for _, number in keys]
        + [block(KEY_ROWS, MOVING_KEYS)] * len(moving)
        + [whole] * len(moving)
        + [block(count, number) for _, number in adds],
        out_specs=[whole] * (n_out + sum(raw)),
        scratch_shapes=[pltpu.VMEM((KEY_ROWS, LANES), jnp.float32)],
        compiler_params=pltpu.CompilerParams(vmem_limit_bytes=VMEM_LIMIT),
        cost_estimate=pl.CostEstimate(flops=weight, bytes_accessed=0, transcendentals=0),
        name=name,
    )(
        place,
        *[array for array, _ in keys],
        *[packed for packed, _ in moving],
        *[packed if parts is None else parts for packed, parts in moving],
        *[array for array, _ in adds],
    )


def pack_kernel(payload, keys, packed):
    packed[pl.ds(0, S_DEV), :] = payload[...]
    packed[pl.ds(S_DEV, KEY_ROWS), :] = keys[...].astype(jnp.float32)


def append_kernel(packed, fetched, longer):
    longer[pl.ds(0, S_DEV + KEY_ROWS), :] = packed[...]
    longer[pl.ds(S_DEV + KEY_ROWS, KEY_ROWS), :] = fetched[...].astype(jnp.float32)


def pack(kernel, name, rows, *arrays):
    whole = pl.BlockSpec(memory_space=pltpu.VMEM)
    return pl.pallas_call(
        kernel,
        out_shape=jax.ShapeDtypeStruct((rows, LANES), jnp.float32),
        in_specs=[whole] * len(arrays),
        out_specs=whole,
        compiler_params=pltpu.CompilerParams(vmem_limit_bytes=VMEM_LIMIT),
        name=name,
    )(*arrays)


def local(resident_keys, moving_keys, payload):
    blocks = lax.axis_size("blk")
    near, far_light, far_heavy, far_heavy_other, fetch, swap, halves = routes(blocks)
    send = lambda array, route: lax.ppermute(array, AXES, route)
    rep = lax.axis_index("rep")
    place = jnp.stack([rep // 2, rep % 2]).astype(jnp.int32)
    own_keys = resident_keys.reshape(KEY_ROWS, LANES)
    home_keys = [(own_keys, 0)]

    first = pack(pack_kernel, "pack", S_DEV + KEY_ROWS, payload, moving_keys.reshape(KEY_ROWS, LANES))
    beside = send(first, near)
    fetched = send(own_keys, fetch)
    mine = pack(append_kernel, "append", S_DEV + 2 * KEY_ROWS, first, fetched)
    theirs = send(mine, swap)
    home, mine_parts = join("home_own", place, home_keys, [(mine, None)], [], (0, 1), weight=HEAVY)
    theirs, home, mine_parts = lax.optimization_barrier((theirs, home, mine_parts))

    far_keys = [(mine, FETCHED_KEYS), (theirs, FETCHED_KEYS)]
    light, theirs_parts = join(
        "light", place, far_keys, [(mine, mine_parts), (theirs, None)], [], (0, 1), second_core=0
    )
    light, theirs_parts, beside = lax.optimization_barrier((light, theirs_parts, beside))
    chip = [(mine, mine_parts), (theirs, theirs_parts)]
    light = send(light, far_light)
    beside_theirs = send(beside, swap)
    (heavy,) = join("heavy_own", place, far_keys, chip, [], (0, 1), second_core=1, weight=HEAVY)
    heavy_same, heavy_other, *beside_parts = join(
        "heavy", place, far_keys, [(beside, None), (beside_theirs, None)], [(heavy, 0)], (0, 1), second_core=1, n_out=2
    )
    heavy_other = send(heavy_other, far_heavy_other)
    rest = list(zip([theirs, beside, beside_theirs], [theirs_parts, *beside_parts]))
    (across,) = join("home_other", place, home_keys, rest, [(home, 1), (light, 1)], (1,))
    across = send(across, halves)
    heavy_same = send(heavy_same, far_heavy)
    (kept,) = join("home_same", place, home_keys, rest, [(home, 0), (light, 0), (heavy_other, 0)], (0,))
    return kept + heavy_same + across


def solution(mesh):
    in_specs = (P("blk"), P(("blk", "rep")), P(("blk", "rep"), None))
    out_specs = P(("blk", "rep"), None)
    return jax.shard_map(local, mesh=mesh, in_specs=in_specs, out_specs=out_specs, check_vma=False)
```

time: 147 us -> 72.5 us (0.49)
  matrix products: 64.7 us -> 0 us
  Pallas kernels: 0 us -> 23.9 us
  blocking collectives: 21.1 us -> 0 us
  starting transfers between devices: 51.5 us -> 37.2 us
  waiting for transfers between devices: 2.47 us -> 7.84 us
  other arithmetic: 2.7 us -> 0.83 us
    dot_general x20 -> x0, matrix products: 64.7 us -> none  [one_block(): jnp.dot(hot, mov_pay, precision=lax.Precision.HIGHEST, preferred_element_...]
    pallas_call x0 -> x8, Pallas kernels: none -> 23.9 us  [the longest x6 20.5 us: join(): pl.pallas_call(functools.partial(join_kernel, len(keys), raw, len(adds),...]
    all_to_all x1 -> x0, blocking collectives: 21.1 us -> none  [summed_on_arrival(): lax.all_to_all(parts, axis, split_axis=0, concat_axis=0, tiled=True)]
    ppermute x8, starting transfers between devices: 51.5 us -> 37.2 us  [local(): send = lambda array, route: lax.ppermute(array, AXES, route)]
    ppermute x8, waiting for transfers between devices: 2.47 us -> 7.84 us  [local(): send = lambda array, route: lax.ppermute(array, AXES, route)]
    another operation x5 -> x0, local copies, waits for them, and re-layouts: 2.31 us -> none
    unnamed x2 -> x8, local copies, waits for them, and re-layouts: 0.01 us -> 1.92 us
  transfers between devices with their start and end apart: 8 -> 8, of which waited for: 1 -> 4; matrix products, arithmetic and copies ran while one was open for 35% -> 0% of each run, Pallas kernels for 0% -> 33%
where the time goes in v1:
time: 72.5 us; the launch traced here: 71.9 us
  starting transfers between devices  37.2 us (51%)
  Pallas kernels  23.9 us (33%)
  waiting for transfers between devices  7.84 us (11%)
  local copies, waits for them, and re-layouts  1.92 us (3%)
  other arithmetic  0.83 us (1%)
    ppermute x8, starting transfers between devices, local(): send = lambda array, route: lax.ppermute(array, AXES, route)  37.2 us
    pallas_call x6, Pallas kernels, join(): pl.pallas_call(functools.partial(join_kernel, len(keys), raw, len(adds),...  20.5 us
    ppermute x8, waiting for transfers between devices, local(): send = lambda array, route: lax.ppermute(array, AXES, route)  7.84 us
    pallas_call x2, Pallas kernels, pack(): pl.pallas_call(kernel, out_shape=jax.ShapeDtypeStruct((rows, LANES), jnp....  3.38 us
    unnamed x8, local copies, waits for them, and re-layouts  1.92 us
  transfers between devices with their start and end apart: 8, of which 4 were waited for; matrix products, arithmetic and copies ran while one was open for 0% of the time, Pallas kernels for 33%

profile of v1, /device:TPU:1, one launch (start us, length us, event | category | flops | bytes accessed | tf_op | source)
XLA Modules:
  0.0 71.9 jit_solution(13721030862571426796)
XLA Ops:
  0.0 14.4 %collective-permute-start = (s32[16,128]{1,0:T(8,128)}, s32[16,128]{1,0:T(8,128)S(1)}, u32[]{:S(2)}, u32[]{:S(2)}) collective-permute-start(s32[16,128]{1,0:T(8,128)} %bitcast.4), channel_id=1, source_target_pairs={{504,0},{9,1},{506,2},{11,3},{12,4},{509,5},{14,6},{511,7},{0,8},{... | collective-permute-start | bytes 24584 | tf_op jit(solution)/shard_map/ppermute | solution.py:150
  14.4 0.0 copy-start
  14.4 1.2 %copy-done = f32[2048,128]{1,0:T(8,128)S(1)} copy-done((f32[2048,128]{1,0:T(8,128)S(1)}, f32[2048,128]{1,0:T(8,128)}, u32[]{:S(2)}) %copy-start) | copy-done | bytes 1048600
  15.6 0.7 copy-done.3
  16.3 1.1 %pack.1.packed = f32[2064,128]{1,0:T(8,128)} custom-call(f32[2048,128]{1,0:T(8,128)S(1)} %copy-done, s32[16,128]{1,0:T(8,128)S(1)} %bitcast.8), custom_call_target="tpu_custom_call" | custom-call | tf_op jit(solution)/shard_map/pack/pallas_call | solution.py:137
  17.4 1.9 %collective-permute-start.2 = (f32[2064,128]{1,0:T(8,128)}, f32[2064,128]{1,0:T(8,128)}, u32[]{:S(2)}, u32[]{:S(2)}) collective-permute-start(f32[2064,128]{1,0:T(8,128)} %pack.1.packed), channel_id=1, source_target_pairs={{0,4},{1,7},{2,6},{3,5},{4,2},{5,1},{6,0},{7,3},{8,12},{9,15},{10,... | collective-permute-start | bytes 3170312 | tf_op jit(solution)/shard_map/ppermute | solution.py:150
  19.3 0.1 pad_add_fusion.refs_0_
  19.4 0.0 collective-permute-done.fetched
  19.4 2.3 %append.1.refs_2_.refs_3_.refs_1_ = f32[2080,128]{1,0:T(8,128)} custom-call(f32[2064,128]{1,0:T(8,128)} %pack.1.packed, s32[16,128]{1,0:T(8,128)S(1)} %collective-permute-done.fetched), custom_call_target="tpu_custom_call" | custom-call | tf_op jit(solution)/shard_map/append/pallas_call | solution.py:137
  21.7 4.3 %collective-permute-start.1 = (f32[2080,128]{1,0:T(8,128)}, f32[2080,128]{1,0:T(8,128)}, u32[]{:S(2)}, u32[]{:S(2)}) collective-permute-start(f32[2080,128]{1,0:T(8,128)} %append.1.refs_2_.refs_3_.refs_1_), channel_id=1, source_target_pairs={{0,1},{1,0},{2,3},{3,2},{4,5},{5,4},{6,7},{7,6},{8,9},{9,8},{10,11... | collective-permute-start | bytes 3194888 | tf_op jit(solution)/shard_map/ppermute | solution.py:150
  26.1 0.0 copy-done.1
  26.1 2.7 %home_own.1 = (f32[1024,128]{1,0:T(8,128)S(1)}, bf16[2048,256]{1,0:T(8,128)(2,1)S(1)}) custom-call(s32[2]{0:T(128)S(1)} %pad_add_fusion.refs_0_, s32[16,128]{1,0:T(8,128)S(1)} %bitcast.5, f32[2080,128]{1,0:T(8,128)} %append.1.refs_2_.refs_3_.refs_1_, f32[2080,128]{1,0:T(8,128)} %append.1.refs_2_.refs_3_.refs_1_), custom_call_target="tpu_custom_call" | custom-call | flops 999999995904 | tf_op jit(solution)/shard_map/home_own/pallas_call | solution.py:102
  28.8 0.0 collective-permute-done.1.refs_2_.refs_4_.refs_6_
  28.8 4.7 %light.1 = (f32[1024,128]{1,0:T(8,128)}, bf16[2048,256]{1,0:T(8,128)(2,1)S(1)}) custom-call(s32[2]{0:T(128)S(1)} %pad_add_fusion.refs_0_, f32[2080,128]{1,0:T(8,128)} %append.1.refs_2_.refs_3_.refs_1_, f32[2080,128]{1,0:T(8,128)} %collective-permute-done.1.refs_2_.refs_4_.refs_6_, f32[2080,128]{1,0:T(8,128)} %append.1.refs_2_.refs_3_.refs_1_, ...), custom_call_target="tpu_custom_call" | custom-call | tf_op jit(solution)/shard_map/light/pallas_call | solution.py:102
  33.5 0.1 collective-permute-done.2.refs_3_.refs_5_
  33.6 2.2 %collective-permute-start.4 = (f32[1024,128]{1,0:T(8,128)}, f32[1024,128]{1,0:T(8,128)}, u32[]{:S(2)}, u32[]{:S(2)}) collective-permute-start(f32[1024,128]{1,0:T(8,128)} %get-tuple-element.30), channel_id=1, source_target_pairs={{0,504},{1,505},{2,506},{3,507},{4,12},{5,13},{6,14},{7,15},{8,0},... | collective-permute-start | bytes 1572872 | tf_op jit(solution)/shard_map/ppermute | solution.py:150
  35.8 4.7 %collective-permute-start.3 = (f32[2064,128]{1,0:T(8,128)}, f32[2064,128]{1,0:T(8,128)}, u32[]{:S(2)}, u32[]{:S(2)}) collective-permute-start(f32[2064,128]{1,0:T(8,128)} %collective-permute-done.2.refs_3_.refs_5_), channel_id=1, source_target_pairs={{0,1},{1,0},{2,3},{3,2},{4,5},{5,4},{6,7},{7,6},{8,9},{9,8},{10,11... | collective-permute-start | bytes 3170312 | tf_op jit(solution)/shard_map/ppermute | solution.py:150
  40.6 3.1 %heavy_own.1.refs_7_ = f32[1024,128]{1,0:T(8,128)S(1)} custom-call(s32[2]{0:T(128)S(1)} %pad_add_fusion.refs_0_, f32[2080,128]{1,0:T(8,128)} %append.1.refs_2_.refs_3_.refs_1_, f32[2080,128]{1,0:T(8,128)} %collective-permute-done.1.refs_2_.refs_4_.refs_6_, f32[2080,128]{1,0:T(8,128)} %append.1.refs_2_.refs_3_.refs_1_, ...), custom_call_target="tpu_custom_call" | custom-call | flops 999999995904 | tf_op jit(solution)/shard_map/heavy_own/pallas_call | solution.py:102
  43.7 0.0 copy-start.2
  43.7 0.0 collective-permute-done.3.refs_4_.refs_6_
  43.7 4.3 %heavy.1 = (f32[512,128]{1,0:T(8,128)S(1)}, f32[512,128]{1,0:T(8,128)S(1)}, bf16[2048,256]{1,0:T(8,128)(2,1)S(1)}, bf16[2048,256]{1,0:T(8,128)(2,1)S(1)}) custom-call(s32[2]{0:T(128)S(1)} %pad_add_fusion.refs_0_, f32[2080,128]{1,0:T(8,128)} %append.1.refs_2_.refs_3_.refs_1_, f32[2080,128]{1,0:T(8,128)} %collective-permute-done.1.refs_2_.refs_4_.refs_6_, ...), custom_call_target="tpu_custom_call" | custom-call | tf_op jit(solution)/shard_map/heavy/pallas_call | solution.py:102
  48.0 3.5 %collective-permute-start.5 = (f32[512,128]{1,0:T(8,128)S(1)}, f32[512,128]{1,0:T(8,128)S(1)}, u32[]{:S(2)}, u32[]{:S(2)}) collective-permute-start(f32[512,128]{1,0:T(8,128)S(1)} %get-tuple-element.31), channel_id=1, source_target_pairs={{0,10},{1,11},{2,8},{3,9},{4,510},{5,511},{6,508},{7,509},{8,18},{... | collective-permute-start | bytes 786440 | tf_op jit(solution)/shard_map/ppermute | solution.py:150
  51.5 0.0 collective-permute-done.4.refs_9_
  51.6 0.0 copy-done.2
  51.6 2.8 %home_other.1 = f32[512,128]{1,0:T(8,128)S(1)} custom-call(s32[2]{0:T(128)S(1)} %pad_add_fusion.refs_0_, s32[16,128]{1,0:T(8,128)S(1)} %bitcast.6, f32[2080,128]{1,0:T(8,128)} %collective-permute-done.1.refs_2_.refs_4_.refs_6_, f32[2064,128]{1,0:T(8,128)} %collective-permute-done.2.refs_3_.refs_5_, f32[2064,128]{1,0:T(8,128)} %collective-permute-done.3.refs_4_.refs_6_, ...), custom_call_target="tpu_custom_call" | custom-call | tf_op jit(solution)/shard_map/home_other/pallas_call | solution.py:102
  54.4 4.2 %collective-permute-start.7 = (f32[512,128]{1,0:T(8,128)S(1)}, f32[512,128]{1,0:T(8,128)S(1)}, u32[]{:S(2)}, u32[]{:S(2)}) collective-permute-start(f32[512,128]{1,0:T(8,128)S(1)} %home_other.1), channel_id=1, source_target_pairs={{0,2},{1,3},{2,0},{3,1},{4,6},{5,7},{6,4},{7,5},{8,10},{9,11},{10,... | collective-permute-start | bytes 786440 | tf_op jit(solution)/shard_map/ppermute | solution.py:150
  58.6 1.9 %collective-permute-start.6 = (f32[512,128]{1,0:T(8,128)S(1)}, f32[512,128]{1,0:T(8,128)S(1)}, u32[]{:S(2)}, u32[]{:S(2)}) collective-permute-start(f32[512,128]{1,0:T(8,128)S(1)} %get-tuple-element.32), channel_id=1, source_target_pairs={{0,8},{1,9},{2,10},{3,11},{4,508},{5,509},{6,510},{7,511},{8,16},{... | collective-permute-start | bytes 786440 | tf_op jit(solution)/shard_map/ppermute | solution.py:150
  60.5 3.0 %collective-permute-done.5.refs_10_ = f32[512,128]{1,0:T(8,128)S(1)} collective-permute-done((f32[512,128]{1,0:T(8,128)S(1)}, f32[512,128]{1,0:T(8,128)S(1)}, u32[]{:S(2)}, u32[]{:S(2)}) %collective-permute-start.5) | collective-permute-done | bytes 262176 | tf_op jit(solution)/shard_map/ppermute | solution.py:150
  63.6 2.8 %home_same.1 = f32[512,128]{1,0:T(8,128)S(1)} custom-call(s32[2]{0:T(128)S(1)} %pad_add_fusion.refs_0_, s32[16,128]{1,0:T(8,128)S(1)} %bitcast.7, f32[2080,128]{1,0:T(8,128)} %collective-permute-done.1.refs_2_.refs_4_.refs_6_, f32[2064,128]{1,0:T(8,128)} %collective-permute-done.2.refs_3_.refs_5_, f32[2064,128]{1,0:T(8,128)} %collective-permute-done.3.refs_4_.refs_6_, ...), custom_call_target="tpu_custom_call" | custom-call | tf_op jit(solution)/shard_map/home_same/pallas_call | solution.py:102
  66.4 3.1 %collective-permute-done.7 = f32[512,128]{1,0:T(8,128)S(1)} collective-permute-done((f32[512,128]{1,0:T(8,128)S(1)}, f32[512,128]{1,0:T(8,128)S(1)}, u32[]{:S(2)}, u32[]{:S(2)}) %collective-permute-start.7) | collective-permute-done | bytes 262176 | tf_op jit(solution)/shard_map/ppermute | solution.py:150
  69.5 1.6 %collective-permute-done.6 = f32[512,128]{1,0:T(8,128)S(1)} collective-permute-done((f32[512,128]{1,0:T(8,128)S(1)}, f32[512,128]{1,0:T(8,128)S(1)}, u32[]{:S(2)}, u32[]{:S(2)}) %collective-permute-start.6) | collective-permute-done | bytes 262176 | tf_op jit(solution)/shard_map/ppermute | solution.py:150
  71.1 0.7 %add_add_fusion = f32[512,128]{1,0:T(8,128)} fusion(f32[512,128]{1,0:T(8,128)S(1)} %collective-permute-done.7, f32[512,128]{1,0:T(8,128)S(1)} %home_same.1, f32[512,128]{1,0:T(8,128)S(1)} %collective-permute-done.6), kind=kLoop, calls=%fused_computation | loop fusion | flops 131072 | bytes 1048576 | tf_op jit(solution)/shard_map/add | solution.py:182
  (2 shorter events, 0.0 us)
Async XLA Ops:
  0.0 19.4 %collective-permute-start = (s32[16,128]{1,0:T(8,128)}, s32[16,128]{1,0:T(8,128)S(1)}, u32[]{:S(2)}, u32[]{:S(2)}) collective-permute-start(s32[16,128]{1,0:T(8,128)} %bitcast.4), channel_id=1, source_target_pairs={{504,0},{9,1},{506,2},{11,3},{12,4},{509,5},{14,6},{511,7},{0,8},{... | collective-permute-start | bytes 24584 | tf_op jit(solution)/shard_map/ppermute | solution.py:150
  14.4 1.2 %copy-start = (f32[2048,128]{1,0:T(8,128)S(1)}, f32[2048,128]{1,0:T(8,128)}, u32[]{:S(2)}) copy-start(f32[2048,128]{1,0:T(8,128)} %payload.1) | copy-start | bytes 3145732
  15.6 0.7 copy-start.3
  17.4 16.2 %collective-permute-start.2 = (f32[2064,128]{1,0:T(8,128)}, f32[2064,128]{1,0:T(8,128)}, u32[]{:S(2)}, u32[]{:S(2)}) collective-permute-start(f32[2064,128]{1,0:T(8,128)} %pack.1.packed), channel_id=1, source_target_pairs={{0,4},{1,7},{2,6},{3,5},{4,2},{5,1},{6,0},{7,3},{8,12},{9,15},{10,... | collective-permute-start | bytes 3170312 | tf_op jit(solution)/shard_map/ppermute | solution.py:150
  19.4 6.6 %copy-start.1 = (s32[2048]{0:T(1024)S(1)}, s32[2048]{0:T(1024)}, u32[]{:S(2)}) copy-start(s32[2048]{0:T(1024)} %param.3) | copy-start | bytes 24580
  21.7 7.1 %collective-permute-start.1 = (f32[2080,128]{1,0:T(8,128)}, f32[2080,128]{1,0:T(8,128)}, u32[]{:S(2)}, u32[]{:S(2)}) collective-permute-start(f32[2080,128]{1,0:T(8,128)} %append.1.refs_2_.refs_3_.refs_1_), channel_id=1, source_target_pairs={{0,1},{1,0},{2,3},{3,2},{4,5},{5,4},{6,7},{7,6},{8,9},{9,8},{10,11... | collective-permute-start | bytes 3194888 | tf_op jit(solution)/shard_map/ppermute | solution.py:150
  33.6 17.9 %collective-permute-start.4 = (f32[1024,128]{1,0:T(8,128)}, f32[1024,128]{1,0:T(8,128)}, u32[]{:S(2)}, u32[]{:S(2)}) collective-permute-start(f32[1024,128]{1,0:T(8,128)} %get-tuple-element.30), channel_id=1, source_target_pairs={{0,504},{1,505},{2,506},{3,507},{4,12},{5,13},{6,14},{7,15},{8,0},... | collective-permute-start | bytes 1572872 | tf_op jit(solution)/shard_map/ppermute | solution.py:150
  35.8 7.9 %collective-permute-start.3 = (f32[2064,128]{1,0:T(8,128)}, f32[2064,128]{1,0:T(8,128)}, u32[]{:S(2)}, u32[]{:S(2)}) collective-permute-start(f32[2064,128]{1,0:T(8,128)} %collective-permute-done.2.refs_3_.refs_5_), channel_id=1, source_target_pairs={{0,1},{1,0},{2,3},{3,2},{4,5},{5,4},{6,7},{7,6},{8,9},{9,8},{10,11... | collective-permute-start | bytes 3170312 | tf_op jit(solution)/shard_map/ppermute | solution.py:150
  43.7 7.8 %copy-start.2 = (s32[2048]{0:T(1024)S(1)}, s32[2048]{0:T(1024)}, u32[]{:S(2)}) copy-start(s32[2048]{0:T(1024)} %param.3) | copy-start | bytes 24580
  48.0 15.5 %collective-permute-start.5 = (f32[512,128]{1,0:T(8,128)S(1)}, f32[512,128]{1,0:T(8,128)S(1)}, u32[]{:S(2)}, u32[]{:S(2)}) collective-permute-start(f32[512,128]{1,0:T(8,128)S(1)} %get-tuple-element.31), channel_id=1, source_target_pairs={{0,10},{1,11},{2,8},{3,9},{4,510},{5,511},{6,508},{7,509},{8,18},{... | collective-permute-start | bytes 786440 | tf_op jit(solution)/shard_map/ppermute | solution.py:150
  54.4 15.1 %collective-permute-start.7 = (f32[512,128]{1,0:T(8,128)S(1)}, f32[512,128]{1,0:T(8,128)S(1)}, u32[]{:S(2)}, u32[]{:S(2)}) collective-permute-start(f32[512,128]{1,0:T(8,128)S(1)} %home_other.1), channel_id=1, source_target_pairs={{0,2},{1,3},{2,0},{3,1},{4,6},{5,7},{6,4},{7,5},{8,10},{9,11},{10,... | collective-permute-start | bytes 786440 | tf_op jit(solution)/shard_map/ppermute | solution.py:150
  58.6 12.5 %collective-permute-start.6 = (f32[512,128]{1,0:T(8,128)S(1)}, f32[512,128]{1,0:T(8,128)S(1)}, u32[]{:S(2)}, u32[]{:S(2)}) collective-permute-start(f32[512,128]{1,0:T(8,128)S(1)} %get-tuple-element.32), channel_id=1, source_target_pairs={{0,8},{1,9},{2,10},{3,11},{4,508},{5,509},{6,510},{7,511},{8,16},{... | collective-permute-start | bytes 786440 | tf_op jit(solution)/shard_map/ppermute | solution.py:150

commit v2 on v1

--- a/solution.py
+++ b/solution.py
@@ -15,7 +15,13 @@
 MOVING_KEYS = S_DEV // KEY_ROWS
 FETCHED_KEYS = MOVING_KEYS + 1
 VMEM_LIMIT = 24 * 1024 * 1024
-HEAVY = 10**12
+W_HOME_OWN = 2 * 10**10
+W_LIGHT = 0
+W_HEAVY_OWN = 0
+W_HOME_THEIRS = 2 * 10**10
+W_HEAVY = 0
+W_HOME_OTHER = 0
+W_HOME_SAME = 0
 
 
 def device(block, half, core, blocks):
@@ -96,6 +102,7 @@
     def block(height, number):
         return pl.BlockSpec((height, LANES), lambda i: (number, 0))
 
+    moved = 4 * LANES * (S_DEV * len(moving) + count * (1 + len(adds)))
     raw = tuple(parts is None for _, parts in moving)
     sums = jax.ShapeDtypeStruct((count // n_out, LANES), jnp.float32)
     split = jax.ShapeDtypeStruct((S_DEV, 2 * LANES), jnp.bfloat16)
@@ -111,7 +118,7 @@
         out_specs=[whole] * (n_out + sum(raw)),
         scratch_shapes=[pltpu.VMEM((KEY_ROWS, LANES), jnp.float32)],
         compiler_params=pltpu.CompilerParams(vmem_limit_bytes=VMEM_LIMIT),
-        cost_estimate=pl.CostEstimate(flops=weight, bytes_accessed=0, transcendentals=0),
+        cost_estimate=pl.CostEstimate(flops=weight + 4 * count * S_DEV * len(moving) * LANES, bytes_accessed=moved, transcendentals=0),
         name=name,
     )(
         place,
@@ -120,28 +127,6 @@
         *[packed if parts is None else parts for packed, parts in moving],
         *[array for array, _ in adds],
     )
-
-
-def pack_kernel(payload, keys, packed):
-    packed[pl.ds(0, S_DEV), :] = payload[...]
-    packed[pl.ds(S_DEV, KEY_ROWS), :] = keys[...].astype(jnp.float32)
-
-
-def append_kernel(packed, fetched, longer):
-    longer[pl.ds(0, S_DEV + KEY_ROWS), :] = packed[...]
-    longer[pl.ds(S_DEV + KEY_ROWS, KEY_ROWS), :] = fetched[...].astype(jnp.float32)
-
-
-def pack(kernel, name, rows, *arrays):
-    whole = pl.BlockSpec(memory_space=pltpu.VMEM)
-    return pl.pallas_call(
-        kernel,
-        out_shape=jax.ShapeDtypeStruct((rows, LANES), jnp.float32),
-        in_specs=[whole] * len(arrays),
-        out_specs=whole,
-        compiler_params=pltpu.CompilerParams(vmem_limit_bytes=VMEM_LIMIT),
-        name=name,
-    )(*arrays)
 
 
 def local(resident_keys, moving_keys, payload):
@@ -153,32 +138,40 @@
     own_keys = resident_keys.reshape(KEY_ROWS, LANES)
     home_keys = [(own_keys, 0)]
 
-    first = pack(pack_kernel, "pack", S_DEV + KEY_ROWS, payload, moving_keys.reshape(KEY_ROWS, LANES))
+    def packed(above, keys):
+        return jnp.concatenate([above, keys.reshape(KEY_ROWS, LANES).astype(jnp.float32)], axis=0)
+
+    fetched = send(own_keys, fetch)
+    first = packed(payload, moving_keys)
     beside = send(first, near)
-    fetched = send(own_keys, fetch)
-    mine = pack(append_kernel, "append", S_DEV + 2 * KEY_ROWS, first, fetched)
+    mine = packed(first, fetched)
     theirs = send(mine, swap)
-    home, mine_parts = join("home_own", place, home_keys, [(mine, None)], [], (0, 1), weight=HEAVY)
+    home, mine_parts = join("home_own", place, home_keys, [(first, None)], [], (0, 1), weight=W_HOME_OWN)
     theirs, home, mine_parts = lax.optimization_barrier((theirs, home, mine_parts))
 
     far_keys = [(mine, FETCHED_KEYS), (theirs, FETCHED_KEYS)]
     light, theirs_parts = join(
-        "light", place, far_keys, [(mine, mine_parts), (theirs, None)], [], (0, 1), second_core=0
+        "light", place, far_keys, [(mine, mine_parts), (theirs, None)], [], (0, 1), second_core=0, weight=W_LIGHT
     )
-    light, theirs_parts, beside = lax.optimization_barrier((light, theirs_parts, beside))
     chip = [(mine, mine_parts), (theirs, theirs_parts)]
     light = send(light, far_light)
+    (heavy,) = join("heavy_own", place, far_keys, chip, [], (0, 1), second_core=1, weight=W_HEAVY_OWN)
+    beside, heavy = lax.optimization_barrier((beside, heavy))
     beside_theirs = send(beside, swap)
-    (heavy,) = join("heavy_own", place, far_keys, chip, [], (0, 1), second_core=1, weight=HEAVY)
+    (home,) = join("home_theirs", place, home_keys, chip[1:], [(home, 0)], (0, 1), weight=W_HOME_THEIRS)
+    beside_theirs, home = lax.optimization_barrier((beside_theirs, home))
     heavy_same, heavy_other, *beside_parts = join(
-        "heavy", place, far_keys, [(beside, None), (beside_theirs, None)], [(heavy, 0)], (0, 1), second_core=1, n_out=2
+        "heavy", place, far_keys, [(beside, None), (beside_theirs, None)], [(heavy, 0)], (0, 1), second_core=1, n_out=2,
+        weight=W_HEAVY,
     )
     heavy_other = send(heavy_other, far_heavy_other)
-    rest = list(zip([theirs, beside, beside_theirs], [theirs_parts, *beside_parts]))
-    (across,) = join("home_other", place, home_keys, rest, [(home, 1), (light, 1)], (1,))
+    rest = list(zip([beside, beside_theirs], beside_parts))
+    (across,) = join("home_other", place, home_keys, rest, [(home, 1), (light, 1)], (1,), weight=W_HOME_OTHER)
     across = send(across, halves)
     heavy_same = send(heavy_same, far_heavy)
-    (kept,) = join("home_same", place, home_keys, rest, [(home, 0), (light, 0), (heavy_other, 0)], (0,))
+    (kept,) = join(
+        "home_same", place, home_keys, rest, [(home, 0), (light, 0), (heavy_other, 0)], (0,), weight=W_HOME_SAME
+    )
     return kept + heavy_same + across
 
 

time: 72.5 us -> 67.6 us (0.932)
  Pallas kernels: 23.9 us -> 16.7 us
  waiting for transfers between devices: 7.84 us -> 10.1 us
  other arithmetic: 0.83 us -> 2.98 us
  local copies, waits for them, and re-layouts: 1.92 us -> 0.01 us
    pallas_call x6 -> x7, Pallas kernels: 20.5 us -> 16.7 us  [join(): pl.pallas_call(functools.partial(join_kernel, len(keys), raw, len(adds),...]
    pallas_call x2 -> x0, Pallas kernels: 3.38 us -> none  [pack(): pl.pallas_call(kernel, out_shape=jax.ShapeDtypeStruct((rows, LANES), jnp....]
    ppermute x8, waiting for transfers between devices: 7.84 us -> 10.1 us  [local(): send = lambda array, route: lax.ppermute(array, AXES, route)]
    unnamed x8 -> x4, local copies, waits for them, and re-layouts: 1.92 us -> 0.01 us
    concatenate x0 -> x2, other arithmetic: none -> 1.45 us  [packed(): jnp.concatenate([above, keys.reshape(KEY_ROWS, LANES).astype(jnp.float32)...]
  transfers between devices with their start and end apart: 8 -> 8, of which waited for: 4 -> 6; matrix products, arithmetic and copies ran while one was open for 0% -> 3% of each run, Pallas kernels for 33% -> 25%
where the time goes in v2:
time: 67.6 us; the launch traced here: 67.2 us
  starting transfers between devices  37.2 us (55%)
  Pallas kernels  16.7 us (25%)
  waiting for transfers between devices  10.1 us (15%)
  other arithmetic  2.98 us (4%)
    ppermute x8, starting transfers between devices, local(): send = lambda array, route: lax.ppermute(array, AXES, route)  37.2 us
    pallas_call x7, Pallas kernels, join(): pl.pallas_call(functools.partial(join_kernel, len(keys), raw, len(adds),...  16.7 us
    ppermute x8, waiting for transfers between devices, local(): send = lambda array, route: lax.ppermute(array, AXES, route)  10.1 us
    concatenate x2, other arithmetic, packed(): jnp.concatenate([above, keys.reshape(KEY_ROWS, LANES).astype(jnp.float32)...  1.45 us
  transfers between devices with their start and end apart: 8, of which 6 were waited for; matrix products, arithmetic and copies ran while one was open for 3% of the time, Pallas kernels for 25%

profile of v2, /device:TPU:1, one launch (start us, length us, event | category | flops | bytes accessed | tf_op | source)
XLA Modules:
  0.0 67.2 jit_solution(36136749121754384)
XLA Ops:
  0.0 14.4 %collective-permute-start.1 = (s32[16,128]{1,0:T(8,128)}, s32[16,128]{1,0:T(8,128)S(1)}, u32[]{:S(2)}, u32[]{:S(2)}) collective-permute-start(s32[16,128]{1,0:T(8,128)} %bitcast.5), channel_id=1, source_target_pairs={{504,0},{9,1},{506,2},{11,3},{12,4},{509,5},{14,6},{511,7},{0,8},{... | collective-permute-start | bytes 24584 | tf_op jit(solution)/shard_map/ppermute | solution.py:135
  14.4 0.7 %convert_bitcast_fusion = f32[16,128]{1,0:T(8,128)S(1)} fusion(s32[2048]{0:T(1024)} %param.4), kind=kLoop, calls=%fused_computation.3 | loop fusion | flops 2048 | bytes 16384 | tf_op jit(solution)/shard_map/convert_element_type | solution.py:142
  15.1 0.0 copy-start.1
  15.1 1.4 %pad_maximum_fusion.1.refs_2_.refs_3_ = f32[2064,128]{1,0:T(8,128)S(1)} fusion(f32[16,128]{1,0:T(8,128)S(1)} %convert_bitcast_fusion, f32[2048,128]{1,0:T(8,128)} %param.5), kind=kLoop, calls=%fused_computation.1 | loop fusion | flops 264192 | bytes 2113536 | tf_op jit(solution)/shard_map/concatenate | solution.py:142
  16.5 1.9 %collective-permute-start = (f32[2064,128]{1,0:T(8,128)S(1)}, f32[2064,128]{1,0:T(8,128)S(1)}, u32[]{:S(2)}, u32[]{:S(2)}) collective-permute-start(f32[2064,128]{1,0:T(8,128)S(1)} %pad_maximum_fusion.1.refs_2_.refs_3_), channel_id=1, source_target_pairs={{0,4},{1,7},{2,6},{3,5},{4,2},{5,1},{6,0},{7,3},{8,12},{9,15},{10,... | collective-permute-start | bytes 3170312 | tf_op jit(solution)/shard_map/ppermute | solution.py:135
  18.4 0.1 pad_add_fusion.refs_0_
  18.5 0.0 collective-permute-done.1
  18.5 0.0 copy-done.1
  18.5 0.0 copy-start
  18.5 0.1 pad_maximum_fusion.refs_1_.refs_3_
  18.6 4.3 %collective-permute-start.2 = (f32[2080,128]{1,0:T(8,128)S(1)}, f32[2080,128]{1,0:T(8,128)S(1)}, u32[]{:S(2)}, u32[]{:S(2)}) collective-permute-start(f32[2080,128]{1,0:T(8,128)S(1)} %pad_maximum_fusion.refs_1_.refs_3_), channel_id=1, source_target_pairs={{0,1},{1,0},{2,3},{3,2},{4,5},{5,4},{6,7},{7,6},{8,9},{9,8},{10,11... | collective-permute-start | bytes 3194888 | tf_op jit(solution)/shard_map/ppermute | solution.py:135
  23.0 0.0 copy-done
  23.0 2.0 %home_own.1 = (f32[1024,128]{1,0:T(8,128)S(1)}, bf16[2048,256]{1,0:T(8,128)(2,1)S(1)}) custom-call(s32[2]{0:T(128)S(1)} %pad_add_fusion.refs_0_, s32[16,128]{1,0:T(8,128)S(1)} %bitcast.6, f32[2064,128]{1,0:T(8,128)S(1)} %pad_maximum_fusion.1.refs_2_.refs_3_, f32[2064,128]{1,0:T(8,128)S(1)} %pad_maximum_fusion.1.refs_2_.refs_3_), custom_call_target="tpu_custom_call" | custom-call | flops 21073741824 | bytes 1572864 | tf_op jit(solution)/shard_map/home_own/pallas_call | solution.py:109
  25.0 0.3 collective-permute-done.2.refs_2_.refs_4_.refs_6_
  25.3 3.1 %light.1 = (f32[1024,128]{1,0:T(8,128)S(1)}, bf16[2048,256]{1,0:T(8,128)(2,1)S(1)}) custom-call(s32[2]{0:T(128)S(1)} %pad_add_fusion.refs_0_, f32[2080,128]{1,0:T(8,128)S(1)} %pad_maximum_fusion.refs_1_.refs_3_, f32[2080,128]{1,0:T(8,128)S(1)} %collective-permute-done.2.refs_2_.refs_4_.refs_6_, f32[2080,128]{1,0:T(8,128)S(1)} %pad_maximum_fusion.refs_1_.refs_3_, ...), custom_call_target="tpu_custom_call" | custom-call | flops 2147483648 | bytes 2621440 | tf_op jit(solution)/shard_map/light/pallas_call | solution.py:109
  28.4 2.9 %heavy_own.1.refs_7_ = f32[1024,128]{1,0:T(8,128)S(1)} custom-call(s32[2]{0:T(128)S(1)} %pad_add_fusion.refs_0_, f32[2080,128]{1,0:T(8,128)S(1)} %pad_maximum_fusion.refs_1_.refs_3_, f32[2080,128]{1,0:T(8,128)S(1)} %collective-permute-done.2.refs_2_.refs_4_.refs_6_, f32[2080,128]{1,0:T(8,128)S(1)} %pad_maximum_fusion.refs_1_.refs_3_, ...), custom_call_target="tpu_custom_call" | custom-call | flops 2147483648 | bytes 2621440 | tf_op jit(solution)/shard_map/heavy_own/pallas_call | solution.py:109
  31.3 1.1 %collective-permute-done.refs_3_.refs_5_.refs_2_ = f32[2064,128]{1,0:T(8,128)S(1)} collective-permute-done((f32[2064,128]{1,0:T(8,128)S(1)}, f32[2064,128]{1,0:T(8,128)S(1)}, u32[]{:S(2)}, u32[]{:S(2)}) %collective-permute-start) | collective-permute-done | bytes 1056800 | tf_op jit(solution)/shard_map/ppermute | solution.py:135
  32.4 2.2 %collective-permute-start.4 = (f32[1024,128]{1,0:T(8,128)S(1)}, f32[1024,128]{1,0:T(8,128)S(1)}, u32[]{:S(2)}, u32[]{:S(2)}) collective-permute-start(f32[1024,128]{1,0:T(8,128)S(1)} %get-tuple-element.32), channel_id=1, source_target_pairs={{0,504},{1,505},{2,506},{3,507},{4,12},{5,13},{6,14},{7,15},{8,0},... | collective-permute-start | bytes 1572872 | tf_op jit(solution)/shard_map/ppermute | solution.py:135
  34.6 4.7 %collective-permute-start.3 = (f32[2064,128]{1,0:T(8,128)S(1)}, f32[2064,128]{1,0:T(8,128)S(1)}, u32[]{:S(2)}, u32[]{:S(2)}) collective-permute-start(f32[2064,128]{1,0:T(8,128)S(1)} %collective-permute-done.refs_3_.refs_5_.refs_2_), channel_id=1, source_target_pairs={{0,1},{1,0},{2,3},{3,2},{4,5},{5,4},{6,7},{7,6},{8,9},{9,8},{10,11... | collective-permute-start | bytes 3170312 | tf_op jit(solution)/shard_map/ppermute | solution.py:135
  39.3 1.8 %home_theirs.1.refs_6_ = f32[1024,128]{1,0:T(8,128)S(1)} custom-call(s32[2]{0:T(128)S(1)} %pad_add_fusion.refs_0_, s32[16,128]{1,0:T(8,128)S(1)} %bitcast.7, f32[2080,128]{1,0:T(8,128)S(1)} %collective-permute-done.2.refs_2_.refs_4_.refs_6_, bf16[2048,256]{1,0:T(8,128)(2,1)S(1)} %get-tuple-element.24.refs_6_.refs_3_, f32[1024,128]{1,0:T(8,128)S(1)} %get-tuple-element.26.refs_4_), custom_call_target="tpu_custom_call" | custom-call | flops 21073741824 | bytes 2097152 | tf_op jit(solution)/shard_map/home_theirs/pallas_call | solution.py:109
  41.2 0.4 collective-permute-done.3.refs_4_.refs_6_.refs_3_
  41.6 3.2 %heavy.1 = (f32[512,128]{1,0:T(8,128)S(1)}, f32[512,128]{1,0:T(8,128)S(1)}, bf16[2048,256]{1,0:T(8,128)(2,1)S(1)}, bf16[2048,256]{1,0:T(8,128)(2,1)S(1)}) custom-call(s32[2]{0:T(128)S(1)} %pad_add_fusion.refs_0_, f32[2080,128]{1,0:T(8,128)S(1)} %pad_maximum_fusion.refs_1_.refs_3_, f32[2080,128]{1,0:T(8,128)S(1)} %collective-permute-done.2.refs_2_.refs_4_.refs_6_, ...), custom_call_target="tpu_custom_call" | custom-call | flops 2147483648 | bytes 3145728 | tf_op jit(solution)/shard_map/heavy/pallas_call | solution.py:109
  44.8 3.5 %collective-permute-start.5 = (f32[512,128]{1,0:T(8,128)S(1)}, f32[512,128]{1,0:T(8,128)S(1)}, u32[]{:S(2)}, u32[]{:S(2)}) collective-permute-start(f32[512,128]{1,0:T(8,128)S(1)} %get-tuple-element.33), channel_id=1, source_target_pairs={{0,10},{1,11},{2,8},{3,9},{4,510},{5,511},{6,508},{7,509},{8,18},{... | collective-permute-start | bytes 786440 | tf_op jit(solution)/shard_map/ppermute | solution.py:135
  48.4 0.0 collective-permute-done.4.refs_7_
  48.4 1.8 %home_other.1 = f32[512,128]{1,0:T(8,128)S(1)} custom-call(s32[2]{0:T(128)S(1)} %pad_add_fusion.refs_0_, s32[16,128]{1,0:T(8,128)S(1)} %bitcast.8, f32[2064,128]{1,0:T(8,128)S(1)} %collective-permute-done.refs_3_.refs_5_.refs_2_, f32[2064,128]{1,0:T(8,128)S(1)} %collective-permute-done.3.refs_4_.refs_6_.refs_3_, ...), custom_call_target="tpu_custom_call" | custom-call | flops 1073741824 | bytes 2883584 | tf_op jit(solution)/shard_map/home_other/pallas_call | solution.py:109
  50.2 4.2 %collective-permute-start.7 = (f32[512,128]{1,0:T(8,128)S(1)}, f32[512,128]{1,0:T(8,128)S(1)}, u32[]{:S(2)}, u32[]{:S(2)}) collective-permute-start(f32[512,128]{1,0:T(8,128)S(1)} %home_other.1), channel_id=1, source_target_pairs={{0,2},{1,3},{2,0},{3,1},{4,6},{5,7},{6,4},{7,5},{8,10},{9,11},{10,... | collective-permute-start | bytes 786440 | tf_op jit(solution)/shard_map/ppermute | solution.py:135
  54.4 1.9 %collective-permute-start.6 = (f32[512,128]{1,0:T(8,128)S(1)}, f32[512,128]{1,0:T(8,128)S(1)}, u32[]{:S(2)}, u32[]{:S(2)}) collective-permute-start(f32[512,128]{1,0:T(8,128)S(1)} %get-tuple-element.34), channel_id=1, source_target_pairs={{0,8},{1,9},{2,10},{3,11},{4,508},{5,509},{6,510},{7,511},{8,16},{... | collective-permute-start | bytes 786440 | tf_op jit(solution)/shard_map/ppermute | solution.py:135
  56.3 3.6 %collective-permute-done.5.refs_8_ = f32[512,128]{1,0:T(8,128)S(1)} collective-permute-done((f32[512,128]{1,0:T(8,128)S(1)}, f32[512,128]{1,0:T(8,128)S(1)}, u32[]{:S(2)}, u32[]{:S(2)}) %collective-permute-start.5) | collective-permute-done | bytes 262176 | tf_op jit(solution)/shard_map/ppermute | solution.py:135
  60.0 1.8 %home_same.1 = f32[512,128]{1,0:T(8,128)S(1)} custom-call(s32[2]{0:T(128)S(1)} %pad_add_fusion.refs_0_, s32[16,128]{1,0:T(8,128)S(1)} %bitcast.9, f32[2064,128]{1,0:T(8,128)S(1)} %collective-permute-done.refs_3_.refs_5_.refs_2_, f32[2064,128]{1,0:T(8,128)S(1)} %collective-permute-done.3.refs_4_.refs_6_.refs_3_, ...), custom_call_target="tpu_custom_call" | custom-call | flops 1073741824 | bytes 3145728 | tf_op jit(solution)/shard_map/home_same/pallas_call | solution.py:109
  61.8 4.5 %collective-permute-done.7 = f32[512,128]{1,0:T(8,128)S(1)} collective-permute-done((f32[512,128]{1,0:T(8,128)S(1)}, f32[512,128]{1,0:T(8,128)S(1)}, u32[]{:S(2)}, u32[]{:S(2)}) %collective-permute-start.7) | collective-permute-done | bytes 262176 | tf_op jit(solution)/shard_map/ppermute | solution.py:135
  66.3 0.2 collective-permute-done.6
  66.5 0.8 %add_add_fusion = f32[512,128]{1,0:T(8,128)} fusion(f32[512,128]{1,0:T(8,128)S(1)} %collective-permute-done.7, f32[512,128]{1,0:T(8,128)S(1)} %home_same.1, f32[512,128]{1,0:T(8,128)S(1)} %collective-permute-done.6), kind=kLoop, calls=%fused_computation.2 | loop fusion | flops 131072 | bytes 1048576 | tf_op jit(solution)/shard_map/add | solution.py:175
  (1 shorter events, 0.0 us)
Async XLA Ops:
  0.0 18.5 %collective-permute-start.1 = (s32[16,128]{1,0:T(8,128)}, s32[16,128]{1,0:T(8,128)S(1)}, u32[]{:S(2)}, u32[]{:S(2)}) collective-permute-start(s32[16,128]{1,0:T(8,128)} %bitcast.5), channel_id=1, source_target_pairs={{504,0},{9,1},{506,2},{11,3},{12,4},{509,5},{14,6},{511,7},{0,8},{... | collective-permute-start | bytes 24584 | tf_op jit(solution)/shard_map/ppermute | solution.py:135
  15.1 3.4 %copy-start.1 = (f32[2048,128]{1,0:T(8,128)S(1)}, f32[2048,128]{1,0:T(8,128)}, u32[]{:S(2)}) copy-start(f32[2048,128]{1,0:T(8,128)} %param.5) | copy-start | bytes 3145732
  16.5 15.9 %collective-permute-start = (f32[2064,128]{1,0:T(8,128)S(1)}, f32[2064,128]{1,0:T(8,128)S(1)}, u32[]{:S(2)}, u32[]{:S(2)}) collective-permute-start(f32[2064,128]{1,0:T(8,128)S(1)} %pad_maximum_fusion.1.refs_2_.refs_3_), channel_id=1, source_target_pairs={{0,4},{1,7},{2,6},{3,5},{4,2},{5,1},{6,0},{7,3},{8,12},{9,15},{10,... | collective-permute-start | bytes 3170312 | tf_op jit(solution)/shard_map/ppermute | solution.py:135
  18.5 4.4 %copy-start = (s32[2048]{0:T(1024)S(1)}, s32[2048]{0:T(1024)}, u32[]{:S(2)}) copy-start(s32[2048]{0:T(1024)} %param.3) | copy-start | bytes 24580
  18.6 6.6 %collective-permute-start.2 = (f32[2080,128]{1,0:T(8,128)S(1)}, f32[2080,128]{1,0:T(8,128)S(1)}, u32[]{:S(2)}, u32[]{:S(2)}) collective-permute-start(f32[2080,128]{1,0:T(8,128)S(1)} %pad_maximum_fusion.refs_1_.refs_3_), channel_id=1, source_target_pairs={{0,1},{1,0},{2,3},{3,2},{4,5},{5,4},{6,7},{7,6},{8,9},{9,8},{10,11... | collective-permute-start | bytes 3194888 | tf_op jit(solution)/shard_map/ppermute | solution.py:135
  32.4 16.0 %collective-permute-start.4 = (f32[1024,128]{1,0:T(8,128)S(1)}, f32[1024,128]{1,0:T(8,128)S(1)}, u32[]{:S(2)}, u32[]{:S(2)}) collective-permute-start(f32[1024,128]{1,0:T(8,128)S(1)} %get-tuple-element.32), channel_id=1, source_target_pairs={{0,504},{1,505},{2,506},{3,507},{4,12},{5,13},{6,14},{7,15},{8,0},... | collective-permute-start | bytes 1572872 | tf_op jit(solution)/shard_map/ppermute | solution.py:135
  34.6 7.0 %collective-permute-start.3 = (f32[2064,128]{1,0:T(8,128)S(1)}, f32[2064,128]{1,0:T(8,128)S(1)}, u32[]{:S(2)}, u32[]{:S(2)}) collective-permute-start(f32[2064,128]{1,0:T(8,128)S(1)} %collective-permute-done.refs_3_.refs_5_.refs_2_), channel_id=1, source_target_pairs={{0,1},{1,0},{2,3},{3,2},{4,5},{5,4},{6,7},{7,6},{8,9},{9,8},{10,11... | collective-permute-start | bytes 3170312 | tf_op jit(solution)/shard_map/ppermute | solution.py:135
  44.8 15.1 %collective-permute-start.5 = (f32[512,128]{1,0:T(8,128)S(1)}, f32[512,128]{1,0:T(8,128)S(1)}, u32[]{:S(2)}, u32[]{:S(2)}) collective-permute-start(f32[512,128]{1,0:T(8,128)S(1)} %get-tuple-element.33), channel_id=1, source_target_pairs={{0,10},{1,11},{2,8},{3,9},{4,510},{5,511},{6,508},{7,509},{8,18},{... | collective-permute-start | bytes 786440 | tf_op jit(solution)/shard_map/ppermute | solution.py:135
  50.2 16.1 %collective-permute-start.7 = (f32[512,128]{1,0:T(8,128)S(1)}, f32[512,128]{1,0:T(8,128)S(1)}, u32[]{:S(2)}, u32[]{:S(2)}) collective-permute-start(f32[512,128]{1,0:T(8,128)S(1)} %home_other.1), channel_id=1, source_target_pairs={{0,2},{1,3},{2,0},{3,1},{4,6},{5,7},{6,4},{7,5},{8,10},{9,11},{10,... | collective-permute-start | bytes 786440 | tf_op jit(solution)/shard_map/ppermute | solution.py:135
  54.4 12.1 %collective-permute-start.6 = (f32[512,128]{1,0:T(8,128)S(1)}, f32[512,128]{1,0:T(8,128)S(1)}, u32[]{:S(2)}, u32[]{:S(2)}) collective-permute-start(f32[512,128]{1,0:T(8,128)S(1)} %get-tuple-element.34), channel_id=1, source_target_pairs={{0,8},{1,9},{2,10},{3,11},{4,508},{5,509},{6,510},{7,511},{8,16},{... | collective-permute-start | bytes 786440 | tf_op jit(solution)/shard_map/ppermute | solution.py:135

commit v3 on v2

v3 whole, which is shorter than its diff:
```python
import functools

import jax
import jax.numpy as jnp
from jax import lax
from jax.experimental import pallas as pl
from jax.experimental.pallas import tpu as pltpu
from jax.sharding import PartitionSpec as P

AXES = ("blk", "rep")
LANES = 128
QUARTER = 512
S_DEV = 2048
KEY_ROWS = 16
MOVING_KEYS = S_DEV // KEY_ROWS
FETCHED_KEYS = MOVING_KEYS + 1
VMEM_LIMIT = 24 * 1024 * 1024
W_HOME_OWN = 2 * 10**10
W_LIGHT = 0
W_HEAVY_OWN = 0
W_HOME_THEIRS = 2 * 10**10
W_HEAVY = 0
W_HOME_OTHER = 0
W_HOME_SAME = 0


def device(block, half, core, blocks):
    return (block % blocks) * 4 + half * 2 + core


def routes(blocks):
    near, far_light, far_heavy, far_heavy_other, fetch, swap, halves = [], [], [], [], [], [], []
    for block in range(blocks):
        low = block % 2
        light = block - 2 if low == 0 else block + 2
        heavy = block + 2 if low == 0 else block - 2
        for half in range(2):
            for core in range(2):
                here = device(block, half, core, blocks)
                x = (half * 2 + low + (1 if core == 0 else -1)) % 4
                near.append((here, device(block - low + x % 2, x // 2, core, blocks)))
                far_light.append((here, device(light, half, core, blocks)))
                far_heavy.append((here, device(heavy, half, core, blocks)))
                far_heavy_other.append((here, device(heavy, 1 - half, core, blocks)))
                fetch.append((device(light if core == 0 else heavy, half, core, blocks), here))
                swap.append((here, device(block, half, 1 - core, blocks)))
                halves.append((here, device(block, 1 - half, core, blocks)))
    return near, far_light, far_heavy, far_heavy_other, fetch, swap, halves


def join_kernel(n_in, keys_at, raw, moving_at, parts_at, adds_at, rows, second_core, n_out, *refs):
    ins, outs, splits = refs[:n_in], refs[n_in : n_in + n_out], list(refs[n_in + n_out : -1])
    keys = refs[-1]
    rep = lax.axis_index("rep")
    half, core = rep // 2, rep % 2

    def key_rows(at):
        operand, block = at
        return ins[operand][pl.ds(block * KEY_ROWS, KEY_ROWS), :].astype(jnp.float32)

    if len(keys_at) == 1:
        keys[...] = key_rows(keys_at[0])
    else:
        keys[...] = jnp.where(core == second_core, key_rows(keys_at[0]), key_rows(keys_at[1]))
    columns = []
    for which in rows:
        quarter = (half if which == 0 else 1 - half) * 2 + core
        for j in range(QUARTER // LANES):
            row = keys[pl.ds(quarter * (QUARTER // LANES) + j, 1), :]
            columns.append(jnp.broadcast_to(row, (LANES, LANES)).T)
    resident = jnp.concatenate(columns, axis=0)
    count = resident.shape[0]
    total = jnp.zeros((count, 2 * LANES), jnp.float32)
    weights = [splits.pop(0) if is_raw else ins[at] for is_raw, at in zip(raw, parts_at)]
    for is_raw, at, split in zip(raw, moving_at, weights):
        if is_raw:
            value = ins[at][pl.ds(0, S_DEV), :]
            high = value.astype(jnp.bfloat16)
            split[:, pl.ds(0, LANES)] = high
            split[:, pl.ds(LANES, LANES)] = (value - high.astype(jnp.float32)).astype(jnp.bfloat16)
    for at, split in zip(moving_at, weights):
        for k in range(S_DEV // 256):
            pieces = []
            for c in range(2):
                mov = ins[at][pl.ds(S_DEV + 2 * k + c, 1), :]
                same = resident == jnp.broadcast_to(mov, (count, LANES))
                pieces.append(jnp.where(same, 1.0, 0.0).astype(jnp.bfloat16))
            hot = jnp.concatenate(pieces, axis=1)
            total = total + jnp.dot(hot, split[pl.ds(256 * k, 256), :], preferred_element_type=jnp.float32)
    joined = total[:, :LANES] + total[:, LANES:]
    for at, block in adds_at:
        joined = joined + ins[at][pl.ds(block * count, count), :]
    each = count // n_out
    for i, out in enumerate(outs):
        out[...] = joined[i * each : (i + 1) * each]


def join(name, keys, moving, adds, rows, second_core=0, n_out=1, weight=0):
    count = QUARTER * len(rows)
    whole = pl.BlockSpec(memory_space=pltpu.VMEM)
    operands = []

    def place(array):
        for at, other in enumerate(operands):
            if other is array:
                return at
        operands.append(array)
        return len(operands) - 1

    keys_at = [(place(array), number) for array, number in keys]
    moving_at = [place(packed) for packed, _ in moving]
    parts_at = [None if parts is None else place(parts) for _, parts in moving]
    adds_at = [(place(array), number) for array, number in adds]
    moved = 4 * LANES * (S_DEV * len(moving) + count * (1 + len(adds)))
    raw = tuple(parts is None for _, parts in moving)
    sums = jax.ShapeDtypeStruct((count // n_out, LANES), jnp.float32)
    split = jax.ShapeDtypeStruct((S_DEV, 2 * LANES), jnp.bfloat16)
    return pl.pallas_call(
        functools.partial(
            join_kernel, len(operands), keys_at, raw, moving_at, parts_at, adds_at, rows, second_core, n_out
        ),
        out_shape=[sums] * n_out + [split] * sum(raw),
        in_specs=[whole] * len(operands),
        out_specs=[whole] * (n_out + sum(raw)),
        scratch_shapes=[pltpu.VMEM((KEY_ROWS, LANES), jnp.float32)],
        compiler_params=pltpu.CompilerParams(vmem_limit_bytes=VMEM_LIMIT),
        cost_estimate=pl.CostEstimate(
            flops=weight + 4 * count * S_DEV * len(moving) * LANES, bytes_accessed=moved, transcendentals=0
        ),
        name=name,
    )(*operands)


def local(resident_keys, moving_keys, payload):
    blocks = lax.axis_size("blk")
    near, far_light, far_heavy, far_heavy_other, fetch, swap, halves = routes(blocks)
    send = lambda array, route: lax.ppermute(array, AXES, route)
    own_keys = resident_keys.reshape(KEY_ROWS, LANES)
    home_keys = [(own_keys, 0)]

    def packed(above, keys):
        return jnp.concatenate([above, keys.reshape(KEY_ROWS, LANES).astype(jnp.float32)], axis=0)

    fetched = send(own_keys, fetch)
    first = packed(payload, moving_keys)
    beside = send(first, near)
    mine = packed(first, fetched)
    theirs = send(mine, swap)
    home, mine_parts = join("home_own", home_keys, [(first, None)], [], (0, 1), weight=W_HOME_OWN)
    theirs, home, mine_parts = lax.optimization_barrier((theirs, home, mine_parts))

    far_keys = [(mine, FETCHED_KEYS), (theirs, FETCHED_KEYS)]
    light, theirs_parts = join(
        "light", far_keys, [(mine, mine_parts), (theirs, None)], [], (0, 1), second_core=0, weight=W_LIGHT
    )
    chip = [(mine, mine_parts), (theirs, theirs_parts)]
    light = send(light, far_light)
    (heavy,) = join("heavy_own", far_keys, chip, [], (0, 1), second_core=1, weight=W_HEAVY_OWN)
    beside, heavy = lax.optimization_barrier((beside, heavy))
    beside_theirs = send(beside, swap)
    (home,) = join("home_theirs", home_keys, chip[1:], [(home, 0)], (0, 1), weight=W_HOME_THEIRS)
    beside_theirs, home = lax.optimization_barrier((beside_theirs, home))
    heavy_same, heavy_other, *beside_parts = join(
        "heavy", far_keys, [(beside, None), (beside_theirs, None)], [(heavy, 0)], (0, 1), second_core=1, n_out=2,
        weight=W_HEAVY,
    )
    heavy_other = send(heavy_other, far_heavy_other)
    rest = list(zip([beside, beside_theirs], beside_parts))
    (across,) = join("home_other", home_keys, rest, [(home, 1), (light, 1)], (1,), weight=W_HOME_OTHER)
    across = send(across, halves)
    heavy_same = send(heavy_same, far_heavy)
    (kept,) = join(
        "home_same", home_keys, rest, [(home, 0), (light, 0), (heavy_other, 0)], (0,), weight=W_HOME_SAME
    )
    return kept + heavy_same + across


def solution(mesh):
    in_specs = (P("blk"), P(("blk", "rep")), P(("blk", "rep"), None))
    out_specs = P(("blk", "rep"), None)
    return jax.shard_map(local, mesh=mesh, in_specs=in_specs, out_specs=out_specs, check_vma=False)
```

time: 67.6 us -> 66.9 us (0.990)
  Pallas kernels: 16.7 us -> 13 us
  waiting for transfers between devices: 10.1 us -> 13.2 us
    pallas_call x7, Pallas kernels: 16.7 us -> 13 us  [join(): pl.pallas_call(functools.partial(join_kernel, len(operands), keys_at, raw...]
    ppermute x8, waiting for transfers between devices: 10.1 us -> 13.2 us  [local(): send = lambda array, route: lax.ppermute(array, AXES, route)]
  transfers between devices with their start and end apart: 8 -> 8, of which waited for: 6 -> 5; matrix products, arithmetic and copies ran while one was open for 3% -> 3% of each run, Pallas kernels for 25% -> 20%
where the time goes in v3:
time: 66.9 us; the launch traced here: 66.5 us
  starting transfers between devices  37.2 us (56%)
  waiting for transfers between devices  13.2 us (20%)
  Pallas kernels  13 us (19%)
  other arithmetic  2.91 us (4%)
    ppermute x8, starting transfers between devices, local(): send = lambda array, route: lax.ppermute(array, AXES, route)  37.2 us
    ppermute x8, waiting for transfers between devices, local(): send = lambda array, route: lax.ppermute(array, AXES, route)  13.2 us
    pallas_call x7, Pallas kernels, join(): pl.pallas_call(functools.partial(join_kernel, len(operands), keys_at, raw...  13 us
    concatenate x2, other arithmetic, packed(): jnp.concatenate([above, keys.reshape(KEY_ROWS, LANES).astype(jnp.float32)...  1.45 us
  transfers between devices with their start and end apart: 8, of which 5 were waited for; matrix products, arithmetic and copies ran while one was open for 3% of the time, Pallas kernels for 20%

profile of v3, /device:TPU:1, one launch (start us, length us, event | category | flops | bytes accessed | tf_op | source)
XLA Modules:
  0.0 66.5 jit_solution(15334211556098732974)
XLA Ops:
  0.0 14.4 %collective-permute-start.1 = (s32[16,128]{1,0:T(8,128)}, s32[16,128]{1,0:T(8,128)S(1)}, u32[]{:S(2)}, u32[]{:S(2)}) collective-permute-start(s32[16,128]{1,0:T(8,128)} %bitcast.3), channel_id=1, source_target_pairs={{504,0},{9,1},{506,2},{11,3},{12,4},{509,5},{14,6},{511,7},{0,8},{... | collective-permute-start | bytes 24584 | tf_op jit(solution)/shard_map/ppermute | solution.py:137
  14.4 0.7 %convert_bitcast_fusion = f32[16,128]{1,0:T(8,128)S(1)} fusion(s32[2048]{0:T(1024)} %param.4), kind=kLoop, calls=%fused_computation.3 | loop fusion | flops 2048 | bytes 16384 | tf_op jit(solution)/shard_map/convert_element_type | solution.py:142
  15.1 0.0 copy-start.1
  15.1 1.4 %pad_maximum_fusion.1.refs_1_ = f32[2064,128]{1,0:T(8,128)S(1)} fusion(f32[16,128]{1,0:T(8,128)S(1)} %convert_bitcast_fusion, f32[2048,128]{1,0:T(8,128)} %param.5), kind=kLoop, calls=%fused_computation.1 | loop fusion | flops 264192 | bytes 2113536 | tf_op jit(solution)/shard_map/concatenate | solution.py:142
  16.5 1.9 %collective-permute-start = (f32[2064,128]{1,0:T(8,128)S(1)}, f32[2064,128]{1,0:T(8,128)S(1)}, u32[]{:S(2)}, u32[]{:S(2)}) collective-permute-start(f32[2064,128]{1,0:T(8,128)S(1)} %pad_maximum_fusion.1.refs_1_), channel_id=1, source_target_pairs={{0,4},{1,7},{2,6},{3,5},{4,2},{5,1},{6,0},{7,3},{8,12},{9,15},{10,... | collective-permute-start | bytes 3170312 | tf_op jit(solution)/shard_map/ppermute | solution.py:137
  18.4 0.0 collective-permute-done.1
  18.4 0.0 copy-done.1
  18.4 0.0 copy-start
  18.5 0.1 pad_maximum_fusion.refs_0_
  18.5 4.3 %collective-permute-start.2 = (f32[2080,128]{1,0:T(8,128)S(1)}, f32[2080,128]{1,0:T(8,128)S(1)}, u32[]{:S(2)}, u32[]{:S(2)}) collective-permute-start(f32[2080,128]{1,0:T(8,128)S(1)} %pad_maximum_fusion.refs_0_), channel_id=1, source_target_pairs={{0,1},{1,0},{2,3},{3,2},{4,5},{5,4},{6,7},{7,6},{8,9},{9,8},{10,11... | collective-permute-start | bytes 3194888 | tf_op jit(solution)/shard_map/ppermute | solution.py:137
  22.9 0.0 copy-done
  22.9 1.4 %home_own.1 = (f32[1024,128]{1,0:T(8,128)S(1)}, bf16[2048,256]{1,0:T(8,128)(2,1)S(1)}) custom-call(s32[16,128]{1,0:T(8,128)S(1)} %bitcast.4, f32[2064,128]{1,0:T(8,128)S(1)} %pad_maximum_fusion.1.refs_1_), custom_call_target="tpu_custom_call" | custom-call | flops 21073741824 | bytes 1572864 | tf_op jit(solution)/shard_map/home_own/pallas_call | solution.py:118
  24.4 0.8 %collective-permute-done.2.refs_1_ = f32[2080,128]{1,0:T(8,128)S(1)} collective-permute-done((f32[2080,128]{1,0:T(8,128)S(1)}, f32[2080,128]{1,0:T(8,128)S(1)}, u32[]{:S(2)}, u32[]{:S(2)}) %collective-permute-start.2) | collective-permute-done | bytes 1064992 | tf_op jit(solution)/shard_map/ppermute | solution.py:137
  25.2 2.6 %light.1 = (f32[1024,128]{1,0:T(8,128)S(1)}, bf16[2048,256]{1,0:T(8,128)(2,1)S(1)}) custom-call(f32[2080,128]{1,0:T(8,128)S(1)} %pad_maximum_fusion.refs_0_, f32[2080,128]{1,0:T(8,128)S(1)} %collective-permute-done.2.refs_1_, bf16[2048,256]{1,0:T(8,128)(2,1)S(1)} %get-tuple-element.23.refs_2_), custom_call_target="tpu_custom_call" | custom-call | flops 2147483648 | bytes 2621440 | tf_op jit(solution)/shard_map/light/pallas_call | solution.py:118
  27.8 2.4 %heavy_own.1.refs_4_ = f32[1024,128]{1,0:T(8,128)S(1)} custom-call(f32[2080,128]{1,0:T(8,128)S(1)} %pad_maximum_fusion.refs_0_, f32[2080,128]{1,0:T(8,128)S(1)} %collective-permute-done.2.refs_1_, bf16[2048,256]{1,0:T(8,128)(2,1)S(1)} %get-tuple-element.23.refs_2_, bf16[2048,256]{1,0:T(8,128)(2,1)S(1)} %get-tuple-element.24.refs_3_.refs_2_), custom_call_target="tpu_custom_call" | custom-call | flops 2147483648 | bytes 2621440 | tf_op jit(solution)/shard_map/heavy_own/pallas_call | solution.py:118
  30.2 2.3 %collective-permute-done.refs_2_.refs_1_ = f32[2064,128]{1,0:T(8,128)S(1)} collective-permute-done((f32[2064,128]{1,0:T(8,128)S(1)}, f32[2064,128]{1,0:T(8,128)S(1)}, u32[]{:S(2)}, u32[]{:S(2)}) %collective-permute-start) | collective-permute-done | bytes 1056800 | tf_op jit(solution)/shard_map/ppermute | solution.py:137
  32.4 2.2 %collective-permute-start.4 = (f32[1024,128]{1,0:T(8,128)S(1)}, f32[1024,128]{1,0:T(8,128)S(1)}, u32[]{:S(2)}, u32[]{:S(2)}) collective-permute-start(f32[1024,128]{1,0:T(8,128)S(1)} %get-tuple-element.32), channel_id=1, source_target_pairs={{0,504},{1,505},{2,506},{3,507},{4,12},{5,13},{6,14},{7,15},{8,0},... | collective-permute-start | bytes 1572872 | tf_op jit(solution)/shard_map/ppermute | solution.py:137
  34.6 4.7 %collective-permute-start.3 = (f32[2064,128]{1,0:T(8,128)S(1)}, f32[2064,128]{1,0:T(8,128)S(1)}, u32[]{:S(2)}, u32[]{:S(2)}) collective-permute-start(f32[2064,128]{1,0:T(8,128)S(1)} %collective-permute-done.refs_2_.refs_1_), channel_id=1, source_target_pairs={{0,1},{1,0},{2,3},{3,2},{4,5},{5,4},{6,7},{7,6},{8,9},{9,8},{10,11... | collective-permute-start | bytes 3170312 | tf_op jit(solution)/shard_map/ppermute | solution.py:137
  39.3 1.3 %home_theirs.1.refs_5_ = f32[1024,128]{1,0:T(8,128)S(1)} custom-call(s32[16,128]{1,0:T(8,128)S(1)} %bitcast.5, f32[2080,128]{1,0:T(8,128)S(1)} %collective-permute-done.2.refs_1_, bf16[2048,256]{1,0:T(8,128)(2,1)S(1)} %get-tuple-element.24.refs_3_.refs_2_, f32[1024,128]{1,0:T(8,128)S(1)} %get-tuple-element.26.refs_3_), custom_call_target="tpu_custom_call" | custom-call | flops 21073741824 | bytes 2097152 | tf_op jit(solution)/shard_map/home_theirs/pallas_call | solution.py:118
  40.7 1.0 %collective-permute-done.3.refs_3_.refs_2_ = f32[2064,128]{1,0:T(8,128)S(1)} collective-permute-done((f32[2064,128]{1,0:T(8,128)S(1)}, f32[2064,128]{1,0:T(8,128)S(1)}, u32[]{:S(2)}, u32[]{:S(2)}) %collective-permute-start.3) | collective-permute-done | bytes 1056800 | tf_op jit(solution)/shard_map/ppermute | solution.py:137
  41.6 2.7 %heavy.1 = (f32[512,128]{1,0:T(8,128)S(1)}, f32[512,128]{1,0:T(8,128)S(1)}, bf16[2048,256]{1,0:T(8,128)(2,1)S(1)}, bf16[2048,256]{1,0:T(8,128)(2,1)S(1)}) custom-call(f32[2080,128]{1,0:T(8,128)S(1)} %pad_maximum_fusion.refs_0_, f32[2080,128]{1,0:T(8,128)S(1)} %collective-permute-done.2.refs_1_, f32[2064,128]{1,0:T(8,128)S(1)} %collective-permute-done.refs_2_.refs_1_, ...), custom_call_target="tpu_custom_call" | custom-call | flops 2147483648 | bytes 3145728 | tf_op jit(solution)/shard_map/heavy/pallas_call | solution.py:118
  44.3 3.5 %collective-permute-start.5 = (f32[512,128]{1,0:T(8,128)S(1)}, f32[512,128]{1,0:T(8,128)S(1)}, u32[]{:S(2)}, u32[]{:S(2)}) collective-permute-start(f32[512,128]{1,0:T(8,128)S(1)} %get-tuple-element.33), channel_id=1, source_target_pairs={{0,10},{1,11},{2,8},{3,9},{4,510},{5,511},{6,508},{7,509},{8,18},{... | collective-permute-start | bytes 786440 | tf_op jit(solution)/shard_map/ppermute | solution.py:137
  47.8 0.0 collective-permute-done.4.refs_6_
  47.9 1.3 %home_other.1 = f32[512,128]{1,0:T(8,128)S(1)} custom-call(s32[16,128]{1,0:T(8,128)S(1)} %bitcast.6, f32[2064,128]{1,0:T(8,128)S(1)} %collective-permute-done.refs_2_.refs_1_, f32[2064,128]{1,0:T(8,128)S(1)} %collective-permute-done.3.refs_3_.refs_2_, bf16[2048,256]{1,0:T(8,128)(2,1)S(1)} %get-tuple-element.29.refs_3_, ...), custom_call_target="tpu_custom_call" | custom-call | flops 1073741824 | bytes 2883584 | tf_op jit(solution)/shard_map/home_other/pallas_call | solution.py:118
  49.2 4.2 %collective-permute-start.7 = (f32[512,128]{1,0:T(8,128)S(1)}, f32[512,128]{1,0:T(8,128)S(1)}, u32[]{:S(2)}, u32[]{:S(2)}) collective-permute-start(f32[512,128]{1,0:T(8,128)S(1)} %home_other.1), channel_id=1, source_target_pairs={{0,2},{1,3},{2,0},{3,1},{4,6},{5,7},{6,4},{7,5},{8,10},{9,11},{10,... | collective-permute-start | bytes 786440 | tf_op jit(solution)/shard_map/ppermute | solution.py:137
  53.4 1.9 %collective-permute-start.6 = (f32[512,128]{1,0:T(8,128)S(1)}, f32[512,128]{1,0:T(8,128)S(1)}, u32[]{:S(2)}, u32[]{:S(2)}) collective-permute-start(f32[512,128]{1,0:T(8,128)S(1)} %get-tuple-element.34), channel_id=1, source_target_pairs={{0,8},{1,9},{2,10},{3,11},{4,508},{5,509},{6,510},{7,511},{8,16},{... | collective-permute-start | bytes 786440 | tf_op jit(solution)/shard_map/ppermute | solution.py:137
  55.3 4.2 %collective-permute-done.5.refs_7_ = f32[512,128]{1,0:T(8,128)S(1)} collective-permute-done((f32[512,128]{1,0:T(8,128)S(1)}, f32[512,128]{1,0:T(8,128)S(1)}, u32[]{:S(2)}, u32[]{:S(2)}) %collective-permute-start.5) | collective-permute-done | bytes 262176 | tf_op jit(solution)/shard_map/ppermute | solution.py:137
  59.4 1.3 %home_same.1 = f32[512,128]{1,0:T(8,128)S(1)} custom-call(s32[16,128]{1,0:T(8,128)S(1)} %bitcast.7, f32[2064,128]{1,0:T(8,128)S(1)} %collective-permute-done.refs_2_.refs_1_, f32[2064,128]{1,0:T(8,128)S(1)} %collective-permute-done.3.refs_3_.refs_2_, bf16[2048,256]{1,0:T(8,128)(2,1)S(1)} %get-tuple-element.29.refs_3_, ...), custom_call_target="tpu_custom_call" | custom-call | flops 1073741824 | bytes 3145728 | tf_op jit(solution)/shard_map/home_same/pallas_call | solution.py:118
  60.8 5.0 %collective-permute-done.7 = f32[512,128]{1,0:T(8,128)S(1)} collective-permute-done((f32[512,128]{1,0:T(8,128)S(1)}, f32[512,128]{1,0:T(8,128)S(1)}, u32[]{:S(2)}, u32[]{:S(2)}) %collective-permute-start.7) | collective-permute-done | bytes 262176 | tf_op jit(solution)/shard_map/ppermute | solution.py:137
  65.8 0.0 collective-permute-done.6
  65.8 0.8 %add_add_fusion = f32[512,128]{1,0:T(8,128)} fusion(f32[512,128]{1,0:T(8,128)S(1)} %collective-permute-done.7, f32[512,128]{1,0:T(8,128)S(1)} %home_same.1, f32[512,128]{1,0:T(8,128)S(1)} %collective-permute-done.6), kind=kLoop, calls=%fused_computation.2 | loop fusion | flops 131072 | bytes 1048576 | tf_op jit(solution)/shard_map/add | solution.py:175
  (1 shorter events, 0.0 us)
Async XLA Ops:
  0.0 18.4 %collective-permute-start.1 = (s32[16,128]{1,0:T(8,128)}, s32[16,128]{1,0:T(8,128)S(1)}, u32[]{:S(2)}, u32[]{:S(2)}) collective-permute-start(s32[16,128]{1,0:T(8,128)} %bitcast.3), channel_id=1, source_target_pairs={{504,0},{9,1},{506,2},{11,3},{12,4},{509,5},{14,6},{511,7},{0,8},{... | collective-permute-start | bytes 24584 | tf_op jit(solution)/shard_map/ppermute | solution.py:137
  15.1 3.3 %copy-start.1 = (f32[2048,128]{1,0:T(8,128)S(1)}, f32[2048,128]{1,0:T(8,128)}, u32[]{:S(2)}) copy-start(f32[2048,128]{1,0:T(8,128)} %param.5) | copy-start | bytes 3145732
  16.5 15.9 %collective-permute-start = (f32[2064,128]{1,0:T(8,128)S(1)}, f32[2064,128]{1,0:T(8,128)S(1)}, u32[]{:S(2)}, u32[]{:S(2)}) collective-permute-start(f32[2064,128]{1,0:T(8,128)S(1)} %pad_maximum_fusion.1.refs_1_), channel_id=1, source_target_pairs={{0,4},{1,7},{2,6},{3,5},{4,2},{5,1},{6,0},{7,3},{8,12},{9,15},{10,... | collective-permute-start | bytes 3170312 | tf_op jit(solution)/shard_map/ppermute | solution.py:137
  18.4 4.4 %copy-start = (s32[2048]{0:T(1024)S(1)}, s32[2048]{0:T(1024)}, u32[]{:S(2)}) copy-start(s32[2048]{0:T(1024)} %param.3) | copy-start | bytes 24580
  18.5 6.6 %collective-permute-start.2 = (f32[2080,128]{1,0:T(8,128)S(1)}, f32[2080,128]{1,0:T(8,128)S(1)}, u32[]{:S(2)}, u32[]{:S(2)}) collective-permute-start(f32[2080,128]{1,0:T(8,128)S(1)} %pad_maximum_fusion.refs_0_), channel_id=1, source_target_pairs={{0,1},{1,0},{2,3},{3,2},{4,5},{5,4},{6,7},{7,6},{8,9},{9,8},{10,11... | collective-permute-start | bytes 3194888 | tf_op jit(solution)/shard_map/ppermute | solution.py:137
  32.4 15.4 %collective-permute-start.4 = (f32[1024,128]{1,0:T(8,128)S(1)}, f32[1024,128]{1,0:T(8,128)S(1)}, u32[]{:S(2)}, u32[]{:S(2)}) collective-permute-start(f32[1024,128]{1,0:T(8,128)S(1)} %get-tuple-element.32), channel_id=1, source_target_pairs={{0,504},{1,505},{2,506},{3,507},{4,12},{5,13},{6,14},{7,15},{8,0},... | collective-permute-start | bytes 1572872 | tf_op jit(solution)/shard_map/ppermute | solution.py:137
  34.6 7.0 %collective-permute-start.3 = (f32[2064,128]{1,0:T(8,128)S(1)}, f32[2064,128]{1,0:T(8,128)S(1)}, u32[]{:S(2)}, u32[]{:S(2)}) collective-permute-start(f32[2064,128]{1,0:T(8,128)S(1)} %collective-permute-done.refs_2_.refs_1_), channel_id=1, source_target_pairs={{0,1},{1,0},{2,3},{3,2},{4,5},{5,4},{6,7},{7,6},{8,9},{9,8},{10,11... | collective-permute-start | bytes 3170312 | tf_op jit(solution)/shard_map/ppermute | solution.py:137
  44.3 15.1 %collective-permute-start.5 = (f32[512,128]{1,0:T(8,128)S(1)}, f32[512,128]{1,0:T(8,128)S(1)}, u32[]{:S(2)}, u32[]{:S(2)}) collective-permute-start(f32[512,128]{1,0:T(8,128)S(1)} %get-tuple-element.33), channel_id=1, source_target_pairs={{0,10},{1,11},{2,8},{3,9},{4,510},{5,511},{6,508},{7,509},{8,18},{... | collective-permute-start | bytes 786440 | tf_op jit(solution)/shard_map/ppermute | solution.py:137
  49.2 16.6 %collective-permute-start.7 = (f32[512,128]{1,0:T(8,128)S(1)}, f32[512,128]{1,0:T(8,128)S(1)}, u32[]{:S(2)}, u32[]{:S(2)}) collective-permute-start(f32[512,128]{1,0:T(8,128)S(1)} %home_other.1), channel_id=1, source_target_pairs={{0,2},{1,3},{2,0},{3,1},{4,6},{5,7},{6,4},{7,5},{8,10},{9,11},{10,... | collective-permute-start | bytes 786440 | tf_op jit(solution)/shard_map/ppermute | solution.py:137
  53.4 12.4 %collective-permute-start.6 = (f32[512,128]{1,0:T(8,128)S(1)}, f32[512,128]{1,0:T(8,128)S(1)}, u32[]{:S(2)}, u32[]{:S(2)}) collective-permute-start(f32[512,128]{1,0:T(8,128)S(1)} %get-tuple-element.34), channel_id=1, source_target_pairs={{0,8},{1,9},{2,10},{3,11},{4,508},{5,509},{6,510},{7,511},{8,16},{... | collective-permute-start | bytes 786440 | tf_op jit(solution)/shard_map/ppermute | solution.py:137

commit v4 on v3

--- a/solution.py
+++ b/solution.py
@@ -19,6 +19,7 @@
 W_LIGHT = 0
 W_HEAVY_OWN = 0
 W_HOME_THEIRS = 2 * 10**10
+W_HEAVY_BESIDE = 2 * 10**10
 W_HEAVY = 0
 W_HOME_OTHER = 0
 W_HOME_SAME = 0
@@ -156,23 +157,26 @@
     chip = [(mine, mine_parts), (theirs, theirs_parts)]
     light = send(light, far_light)
     (heavy,) = join("heavy_own", far_keys, chip, [], (0, 1), second_core=1, weight=W_HEAVY_OWN)
-    beside, heavy = lax.optimization_barrier((beside, heavy))
+    (home,) = join("home_theirs", home_keys, chip[1:], [(home, 0)], (0, 1), weight=W_HOME_THEIRS)
+    beside, heavy, home = lax.optimization_barrier((beside, heavy, home))
     beside_theirs = send(beside, swap)
-    (home,) = join("home_theirs", home_keys, chip[1:], [(home, 0)], (0, 1), weight=W_HOME_THEIRS)
-    beside_theirs, home = lax.optimization_barrier((beside_theirs, home))
-    heavy_same, heavy_other, *beside_parts = join(
-        "heavy", far_keys, [(beside, None), (beside_theirs, None)], [(heavy, 0)], (0, 1), second_core=1, n_out=2,
-        weight=W_HEAVY,
+    heavy, *beside_parts = join(
+        "heavy_beside", far_keys, [(beside, None)], [(heavy, 0)], (0, 1), second_core=1, weight=W_HEAVY_BESIDE
     )
+    beside_theirs, heavy = lax.optimization_barrier((beside_theirs, heavy))
+    heavy_same, heavy_other, *more_parts = join(
+        "heavy", far_keys, [(beside_theirs, None)], [(heavy, 0)], (0, 1), second_core=1, n_out=2, weight=W_HEAVY
+    )
+    beside_parts = beside_parts + more_parts
     heavy_other = send(heavy_other, far_heavy_other)
     rest = list(zip([beside, beside_theirs], beside_parts))
     (across,) = join("home_other", home_keys, rest, [(home, 1), (light, 1)], (1,), weight=W_HOME_OTHER)
     across = send(across, halves)
     heavy_same = send(heavy_same, far_heavy)
     (kept,) = join(
-        "home_same", home_keys, rest, [(home, 0), (light, 0), (heavy_other, 0)], (0,), weight=W_HOME_SAME
+        "home_same", home_keys, rest, [(home, 0), (light, 0), (heavy_other, 0), (heavy_same, 0)], (0,), weight=W_HOME_SAME
     )
-    return kept + heavy_same + across
+    return kept + across
 
 
 def solution(mesh):

time: 66.9 us -> 65.7 us (0.982)
  waiting for transfers between devices: 13.2 us -> 11.8 us
    ppermute x8, waiting for transfers between devices: 13.2 us -> 11.8 us  [local(): send = lambda array, route: lax.ppermute(array, AXES, route)]
    pallas_call x7 -> x8, Pallas kernels: 13 us -> 13.3 us  [join(): pl.pallas_call(functools.partial(join_kernel, len(operands), keys_at, raw...]
  transfers between devices with their start and end apart: 8 -> 8, of which waited for: 5 -> 6; matrix products, arithmetic and copies ran while one was open for 3% -> 3% of each run, Pallas kernels for 20% -> 20%
where the time goes in v4:
time: 65.7 us; the launch traced here: 65.3 us
  starting transfers between devices  37.2 us (57%)
  Pallas kernels  13.3 us (20%)
  waiting for transfers between devices  11.8 us (18%)
  other arithmetic  2.89 us (4%)
    ppermute x8, starting transfers between devices, local(): send = lambda array, route: lax.ppermute(array, AXES, route)  37.2 us
    pallas_call x8, Pallas kernels, join(): pl.pallas_call(functools.partial(join_kernel, len(operands), keys_at, raw...  13.3 us
    ppermute x8, waiting for transfers between devices, local(): send = lambda array, route: lax.ppermute(array, AXES, route)  11.8 us
    concatenate x2, other arithmetic, packed(): jnp.concatenate([above, keys.reshape(KEY_ROWS, LANES).astype(jnp.float32)...  1.45 us
  transfers between devices with their start and end apart: 8, of which 6 were waited for; matrix products, arithmetic and copies ran while one was open for 3% of the time, Pallas kernels for 20%

profile of v4, /device:TPU:1, one launch (start us, length us, event | category | flops | bytes accessed | tf_op | source)
XLA Modules:
  0.0 65.3 jit_solution(607389107609265352)
XLA Ops:
  0.0 14.4 %collective-permute-start.1 = (s32[16,128]{1,0:T(8,128)}, s32[16,128]{1,0:T(8,128)S(1)}, u32[]{:S(2)}, u32[]{:S(2)}) collective-permute-start(s32[16,128]{1,0:T(8,128)} %bitcast.3), channel_id=1, source_target_pairs={{504,0},{9,1},{506,2},{11,3},{12,4},{509,5},{14,6},{511,7},{0,8},{... | collective-permute-start | bytes 24584 | tf_op jit(solution)/shard_map/ppermute | solution.py:138
  14.4 0.7 %convert_bitcast_fusion = f32[16,128]{1,0:T(8,128)S(1)} fusion(s32[2048]{0:T(1024)} %param.4), kind=kLoop, calls=%fused_computation.2 | loop fusion | flops 2048 | bytes 16384 | tf_op jit(solution)/shard_map/convert_element_type | solution.py:143
  15.1 0.0 copy-start.1
  15.1 1.4 %pad_maximum_fusion.1.refs_1_ = f32[2064,128]{1,0:T(8,128)S(1)} fusion(f32[16,128]{1,0:T(8,128)S(1)} %convert_bitcast_fusion, f32[2048,128]{1,0:T(8,128)} %param.5), kind=kLoop, calls=%fused_computation.1 | loop fusion | flops 264192 | bytes 2113536 | tf_op jit(solution)/shard_map/concatenate | solution.py:143
  16.5 1.9 %collective-permute-start = (f32[2064,128]{1,0:T(8,128)S(1)}, f32[2064,128]{1,0:T(8,128)S(1)}, u32[]{:S(2)}, u32[]{:S(2)}) collective-permute-start(f32[2064,128]{1,0:T(8,128)S(1)} %pad_maximum_fusion.1.refs_1_), channel_id=1, source_target_pairs={{0,4},{1,7},{2,6},{3,5},{4,2},{5,1},{6,0},{7,3},{8,12},{9,15},{10,... | collective-permute-start | bytes 3170312 | tf_op jit(solution)/shard_map/ppermute | solution.py:138
  18.4 0.0 collective-permute-done.1
  18.4 0.0 copy-done.1
  18.4 0.0 copy-start
  18.5 0.1 pad_maximum_fusion.refs_0_
  18.5 4.3 %collective-permute-start.2 = (f32[2080,128]{1,0:T(8,128)S(1)}, f32[2080,128]{1,0:T(8,128)S(1)}, u32[]{:S(2)}, u32[]{:S(2)}) collective-permute-start(f32[2080,128]{1,0:T(8,128)S(1)} %pad_maximum_fusion.refs_0_), channel_id=1, source_target_pairs={{0,1},{1,0},{2,3},{3,2},{4,5},{5,4},{6,7},{7,6},{8,9},{9,8},{10,11... | collective-permute-start | bytes 3194888 | tf_op jit(solution)/shard_map/ppermute | solution.py:138
  22.9 0.0 copy-done
  22.9 1.4 %home_own.1 = (f32[1024,128]{1,0:T(8,128)S(1)}, bf16[2048,256]{1,0:T(8,128)(2,1)S(1)}) custom-call(s32[16,128]{1,0:T(8,128)S(1)} %bitcast.4, f32[2064,128]{1,0:T(8,128)S(1)} %pad_maximum_fusion.1.refs_1_), custom_call_target="tpu_custom_call" | custom-call | flops 21073741824 | bytes 1572864 | tf_op jit(solution)/shard_map/home_own/pallas_call | solution.py:119
  24.4 0.8 %collective-permute-done.2.refs_1_ = f32[2080,128]{1,0:T(8,128)S(1)} collective-permute-done((f32[2080,128]{1,0:T(8,128)S(1)}, f32[2080,128]{1,0:T(8,128)S(1)}, u32[]{:S(2)}, u32[]{:S(2)}) %collective-permute-start.2) | collective-permute-done | bytes 1064992 | tf_op jit(solution)/shard_map/ppermute | solution.py:138
  25.2 2.6 %light.1 = (f32[1024,128]{1,0:T(8,128)S(1)}, bf16[2048,256]{1,0:T(8,128)(2,1)S(1)}) custom-call(f32[2080,128]{1,0:T(8,128)S(1)} %pad_maximum_fusion.refs_0_, f32[2080,128]{1,0:T(8,128)S(1)} %collective-permute-done.2.refs_1_, bf16[2048,256]{1,0:T(8,128)(2,1)S(1)} %get-tuple-element.25.refs_2_), custom_call_target="tpu_custom_call" | custom-call | flops 2147483648 | bytes 2621440 | tf_op jit(solution)/shard_map/light/pallas_call | solution.py:119
  27.8 1.3 %home_theirs.1.refs_5_ = f32[1024,128]{1,0:T(8,128)S(1)} custom-call(s32[16,128]{1,0:T(8,128)S(1)} %bitcast.5, f32[2080,128]{1,0:T(8,128)S(1)} %collective-permute-done.2.refs_1_, bf16[2048,256]{1,0:T(8,128)(2,1)S(1)} %get-tuple-element.26.refs_3_.refs_2_, f32[1024,128]{1,0:T(8,128)S(1)} %get-tuple-element.27.refs_3_), custom_call_target="tpu_custom_call" | custom-call | flops 21073741824 | bytes 2097152 | tf_op jit(solution)/shard_map/home_theirs/pallas_call | solution.py:119
  29.1 2.4 %heavy_own.1.refs_3_ = f32[1024,128]{1,0:T(8,128)S(1)} custom-call(f32[2080,128]{1,0:T(8,128)S(1)} %pad_maximum_fusion.refs_0_, f32[2080,128]{1,0:T(8,128)S(1)} %collective-permute-done.2.refs_1_, bf16[2048,256]{1,0:T(8,128)(2,1)S(1)} %get-tuple-element.25.refs_2_, bf16[2048,256]{1,0:T(8,128)(2,1)S(1)} %get-tuple-element.26.refs_3_.refs_2_), custom_call_target="tpu_custom_call" | custom-call | flops 2147483648 | bytes 2621440 | tf_op jit(solution)/shard_map/heavy_own/pallas_call | solution.py:119
  31.5 0.9 %collective-permute-done.refs_2_.refs_1_ = f32[2064,128]{1,0:T(8,128)S(1)} collective-permute-done((f32[2064,128]{1,0:T(8,128)S(1)}, f32[2064,128]{1,0:T(8,128)S(1)}, u32[]{:S(2)}, u32[]{:S(2)}) %collective-permute-start) | collective-permute-done | bytes 1056800 | tf_op jit(solution)/shard_map/ppermute | solution.py:138
  32.4 2.2 %collective-permute-start.4 = (f32[1024,128]{1,0:T(8,128)S(1)}, f32[1024,128]{1,0:T(8,128)S(1)}, u32[]{:S(2)}, u32[]{:S(2)}) collective-permute-start(f32[1024,128]{1,0:T(8,128)S(1)} %get-tuple-element.36), channel_id=1, source_target_pairs={{0,504},{1,505},{2,506},{3,507},{4,12},{5,13},{6,14},{7,15},{8,0},... | collective-permute-start | bytes 1572872 | tf_op jit(solution)/shard_map/ppermute | solution.py:138
  34.6 4.7 %collective-permute-start.3 = (f32[2064,128]{1,0:T(8,128)S(1)}, f32[2064,128]{1,0:T(8,128)S(1)}, u32[]{:S(2)}, u32[]{:S(2)}) collective-permute-start(f32[2064,128]{1,0:T(8,128)S(1)} %collective-permute-done.refs_2_.refs_1_), channel_id=1, source_target_pairs={{0,1},{1,0},{2,3},{3,2},{4,5},{5,4},{6,7},{7,6},{8,9},{9,8},{10,11... | collective-permute-start | bytes 3170312 | tf_op jit(solution)/shard_map/ppermute | solution.py:138
  39.3 1.4 %heavy_beside.1 = (f32[1024,128]{1,0:T(8,128)S(1)}, bf16[2048,256]{1,0:T(8,128)(2,1)S(1)}) custom-call(f32[2080,128]{1,0:T(8,128)S(1)} %pad_maximum_fusion.refs_0_, f32[2080,128]{1,0:T(8,128)S(1)} %collective-permute-done.2.refs_1_, f32[2064,128]{1,0:T(8,128)S(1)} %collective-permute-done.refs_2_.refs_1_, f32[1024,128]{1,0:T(8,128)S(1)} %heavy_own.1.refs_3_), custom_call_target="tpu_custom_call" | custom-call | flops 21073741824 | bytes 2097152 | tf_op jit(solution)/shard_map/heavy_beside/pallas_call | solution.py:119
  40.8 0.8 %collective-permute-done.3.refs_2_ = f32[2064,128]{1,0:T(8,128)S(1)} collective-permute-done((f32[2064,128]{1,0:T(8,128)S(1)}, f32[2064,128]{1,0:T(8,128)S(1)}, u32[]{:S(2)}, u32[]{:S(2)}) %collective-permute-start.3) | collective-permute-done | bytes 1056800 | tf_op jit(solution)/shard_map/ppermute | solution.py:138
  41.6 1.5 %heavy.1 = (f32[512,128]{1,0:T(8,128)S(1)}, f32[512,128]{1,0:T(8,128)S(1)}, bf16[2048,256]{1,0:T(8,128)(2,1)S(1)}) custom-call(f32[2080,128]{1,0:T(8,128)S(1)} %pad_maximum_fusion.refs_0_, f32[2080,128]{1,0:T(8,128)S(1)} %collective-permute-done.2.refs_1_, f32[2064,128]{1,0:T(8,128)S(1)} %collective-permute-done.3.refs_2_, ...), custom_call_target="tpu_custom_call" | custom-call | flops 1073741824 | bytes 2097152 | tf_op jit(solution)/shard_map/heavy/pallas_call | solution.py:119
  43.1 3.5 %collective-permute-start.5 = (f32[512,128]{1,0:T(8,128)S(1)}, f32[512,128]{1,0:T(8,128)S(1)}, u32[]{:S(2)}, u32[]{:S(2)}) collective-permute-start(f32[512,128]{1,0:T(8,128)S(1)} %get-tuple-element.37), channel_id=1, source_target_pairs={{0,10},{1,11},{2,8},{3,9},{4,510},{5,511},{6,508},{7,509},{8,18},{... | collective-permute-start | bytes 786440 | tf_op jit(solution)/shard_map/ppermute | solution.py:138
  46.6 1.9 %collective-permute-start.6 = (f32[512,128]{1,0:T(8,128)S(1)}, f32[512,128]{1,0:T(8,128)S(1)}, u32[]{:S(2)}, u32[]{:S(2)}) collective-permute-start(f32[512,128]{1,0:T(8,128)S(1)} %get-tuple-element.38), channel_id=1, source_target_pairs={{0,8},{1,9},{2,10},{3,11},{4,508},{5,509},{6,510},{7,511},{8,16},{... | collective-permute-start | bytes 786440 | tf_op jit(solution)/shard_map/ppermute | solution.py:138
  48.5 0.0 collective-permute-done.4.refs_6_
  48.6 1.3 %home_other.1 = f32[512,128]{1,0:T(8,128)S(1)} custom-call(s32[16,128]{1,0:T(8,128)S(1)} %bitcast.6, f32[2064,128]{1,0:T(8,128)S(1)} %collective-permute-done.refs_2_.refs_1_, f32[2064,128]{1,0:T(8,128)S(1)} %collective-permute-done.3.refs_2_, bf16[2048,256]{1,0:T(8,128)(2,1)S(1)} %get-tuple-element.32.refs_3_, ...), custom_call_target="tpu_custom_call" | custom-call | flops 1073741824 | bytes 2883584 | tf_op jit(solution)/shard_map/home_other/pallas_call | solution.py:119
  49.9 4.2 %collective-permute-start.7 = (f32[512,128]{1,0:T(8,128)S(1)}, f32[512,128]{1,0:T(8,128)S(1)}, u32[]{:S(2)}, u32[]{:S(2)}) collective-permute-start(f32[512,128]{1,0:T(8,128)S(1)} %home_other.1), channel_id=1, source_target_pairs={{0,2},{1,3},{2,0},{3,1},{4,6},{5,7},{6,4},{7,5},{8,10},{9,11},{10,... | collective-permute-start | bytes 786440 | tf_op jit(solution)/shard_map/ppermute | solution.py:138
  54.0 4.2 %collective-permute-done.5.refs_7_ = f32[512,128]{1,0:T(8,128)S(1)} collective-permute-done((f32[512,128]{1,0:T(8,128)S(1)}, f32[512,128]{1,0:T(8,128)S(1)}, u32[]{:S(2)}, u32[]{:S(2)}) %collective-permute-start.5) | collective-permute-done | bytes 262176 | tf_op jit(solution)/shard_map/ppermute | solution.py:138
  58.2 4.4 %collective-permute-done.6.refs_8_ = f32[512,128]{1,0:T(8,128)S(1)} collective-permute-done((f32[512,128]{1,0:T(8,128)S(1)}, f32[512,128]{1,0:T(8,128)S(1)}, u32[]{:S(2)}, u32[]{:S(2)}) %collective-permute-start.6) | collective-permute-done | bytes 262176 | tf_op jit(solution)/shard_map/ppermute | solution.py:138
  62.6 1.3 %home_same.1 = f32[512,128]{1,0:T(8,128)S(1)} custom-call(s32[16,128]{1,0:T(8,128)S(1)} %bitcast.7, f32[2064,128]{1,0:T(8,128)S(1)} %collective-permute-done.refs_2_.refs_1_, f32[2064,128]{1,0:T(8,128)S(1)} %collective-permute-done.3.refs_2_, bf16[2048,256]{1,0:T(8,128)(2,1)S(1)} %get-tuple-element.32.refs_3_, ...), custom_call_target="tpu_custom_call" | custom-call | flops 1073741824 | bytes 3407872 | tf_op jit(solution)/shard_map/home_same/pallas_call | solution.py:119
  63.9 0.6 collective-permute-done.7
  64.5 0.7 %add.3 = f32[512,128]{1,0:T(8,128)} add(f32[512,128]{1,0:T(8,128)S(1)} %home_same.1, f32[512,128]{1,0:T(8,128)S(1)} %collective-permute-done.7) | non-fusion elementwise | flops 65536 | bytes 786432 | tf_op jit(solution)/shard_map/add | solution.py:179
  (1 shorter events, 0.0 us)
Async XLA Ops:
  0.0 18.4 %collective-permute-start.1 = (s32[16,128]{1,0:T(8,128)}, s32[16,128]{1,0:T(8,128)S(1)}, u32[]{:S(2)}, u32[]{:S(2)}) collective-permute-start(s32[16,128]{1,0:T(8,128)} %bitcast.3), channel_id=1, source_target_pairs={{504,0},{9,1},{506,2},{11,3},{12,4},{509,5},{14,6},{511,7},{0,8},{... | collective-permute-start | bytes 24584 | tf_op jit(solution)/shard_map/ppermute | solution.py:138
  15.1 3.3 %copy-start.1 = (f32[2048,128]{1,0:T(8,128)S(1)}, f32[2048,128]{1,0:T(8,128)}, u32[]{:S(2)}) copy-start(f32[2048,128]{1,0:T(8,128)} %param.5) | copy-start | bytes 3145732
  16.5 15.9 %collective-permute-start = (f32[2064,128]{1,0:T(8,128)S(1)}, f32[2064,128]{1,0:T(8,128)S(1)}, u32[]{:S(2)}, u32[]{:S(2)}) collective-permute-start(f32[2064,128]{1,0:T(8,128)S(1)} %pad_maximum_fusion.1.refs_1_), channel_id=1, source_target_pairs={{0,4},{1,7},{2,6},{3,5},{4,2},{5,1},{6,0},{7,3},{8,12},{9,15},{10,... | collective-permute-start | bytes 3170312 | tf_op jit(solution)/shard_map/ppermute | solution.py:138
  18.4 4.4 %copy-start = (s32[2048]{0:T(1024)S(1)}, s32[2048]{0:T(1024)}, u32[]{:S(2)}) copy-start(s32[2048]{0:T(1024)} %param.3) | copy-start | bytes 24580
  18.5 6.6 %collective-permute-start.2 = (f32[2080,128]{1,0:T(8,128)S(1)}, f32[2080,128]{1,0:T(8,128)S(1)}, u32[]{:S(2)}, u32[]{:S(2)}) collective-permute-start(f32[2080,128]{1,0:T(8,128)S(1)} %pad_maximum_fusion.refs_0_), channel_id=1, source_target_pairs={{0,1},{1,0},{2,3},{3,2},{4,5},{5,4},{6,7},{7,6},{8,9},{9,8},{10,11... | collective-permute-start | bytes 3194888 | tf_op jit(solution)/shard_map/ppermute | solution.py:138
  32.4 16.1 %collective-permute-start.4 = (f32[1024,128]{1,0:T(8,128)S(1)}, f32[1024,128]{1,0:T(8,128)S(1)}, u32[]{:S(2)}, u32[]{:S(2)}) collective-permute-start(f32[1024,128]{1,0:T(8,128)S(1)} %get-tuple-element.36), channel_id=1, source_target_pairs={{0,504},{1,505},{2,506},{3,507},{4,12},{5,13},{6,14},{7,15},{8,0},... | collective-permute-start | bytes 1572872 | tf_op jit(solution)/shard_map/ppermute | solution.py:138
  34.6 7.0 %collective-permute-start.3 = (f32[2064,128]{1,0:T(8,128)S(1)}, f32[2064,128]{1,0:T(8,128)S(1)}, u32[]{:S(2)}, u32[]{:S(2)}) collective-permute-start(f32[2064,128]{1,0:T(8,128)S(1)} %collective-permute-done.refs_2_.refs_1_), channel_id=1, source_target_pairs={{0,1},{1,0},{2,3},{3,2},{4,5},{5,4},{6,7},{7,6},{8,9},{9,8},{10,11... | collective-permute-start | bytes 3170312 | tf_op jit(solution)/shard_map/ppermute | solution.py:138
  43.1 15.1 %collective-permute-start.5 = (f32[512,128]{1,0:T(8,128)S(1)}, f32[512,128]{1,0:T(8,128)S(1)}, u32[]{:S(2)}, u32[]{:S(2)}) collective-permute-start(f32[512,128]{1,0:T(8,128)S(1)} %get-tuple-element.37), channel_id=1, source_target_pairs={{0,10},{1,11},{2,8},{3,9},{4,510},{5,511},{6,508},{7,509},{8,18},{... | collective-permute-start | bytes 786440 | tf_op jit(solution)/shard_map/ppermute | solution.py:138
  46.6 16.0 %collective-permute-start.6 = (f32[512,128]{1,0:T(8,128)S(1)}, f32[512,128]{1,0:T(8,128)S(1)}, u32[]{:S(2)}, u32[]{:S(2)}) collective-permute-start(f32[512,128]{1,0:T(8,128)S(1)} %get-tuple-element.38), channel_id=1, source_target_pairs={{0,8},{1,9},{2,10},{3,11},{4,508},{5,509},{6,510},{7,511},{8,16},{... | collective-permute-start | bytes 786440 | tf_op jit(solution)/shard_map/ppermute | solution.py:138
  49.9 14.7 %collective-permute-start.7 = (f32[512,128]{1,0:T(8,128)S(1)}, f32[512,128]{1,0:T(8,128)S(1)}, u32[]{:S(2)}, u32[]{:S(2)}) collective-permute-start(f32[512,128]{1,0:T(8,128)S(1)} %home_other.1), channel_id=1, source_target_pairs={{0,2},{1,3},{2,0},{3,1},{4,6},{5,7},{6,4},{7,5},{8,10},{9,11},{10,... | collective-permute-start | bytes 786440 | tf_op jit(solution)/shard_map/ppermute | solution.py:138

commit v5 on v4

--- a/solution.py
+++ b/solution.py
@@ -143,7 +143,8 @@
         return jnp.concatenate([above, keys.reshape(KEY_ROWS, LANES).astype(jnp.float32)], axis=0)
 
     fetched = send(own_keys, fetch)
-    first = packed(payload, moving_keys)
+    key_rows = jnp.pad(moving_keys.reshape(KEY_ROWS, LANES), ((S_DEV, 0), (0, 0))).astype(jnp.float32)
+    first = jnp.pad(payload, ((0, KEY_ROWS), (0, 0))) + key_rows
     beside = send(first, near)
     mine = packed(first, fetched)
     theirs = send(mine, swap)

time: 65.7 us -> 64.9 us (0.988)
  other arithmetic: 2.89 us -> 2.13 us
    concatenate x2 -> x1, other arithmetic: 1.45 us -> 0.07 us  [packed(): jnp.concatenate([above, keys.reshape(KEY_ROWS, LANES).astype(jnp.float32)...]
    add x0 -> x1, other arithmetic: none -> 1.31 us  [local(): first = jnp.pad(payload, ((0, KEY_ROWS), (0, 0))) + key_rows]
    convert_element_type x2 -> x1, other arithmetic: 0.7 us -> 0.01 us  [packed(): keys.reshape(KEY_ROWS, LANES).astype(jnp.float32)]
  transfers between devices with their start and end apart: 8 -> 8, of which waited for: 6 -> 6; matrix products, arithmetic and copies ran while one was open for 3% -> 2% of each run, Pallas kernels for 20% -> 20%
where the time goes in v5:
time: 64.9 us; the launch traced here: 64.5 us
  starting transfers between devices  37.2 us (57%)
  Pallas kernels  13.2 us (20%)
  waiting for transfers between devices  11.8 us (18%)
  other arithmetic  2.13 us (3%)
    ppermute x8, starting transfers between devices, local(): send = lambda array, route: lax.ppermute(array, AXES, route)  37.2 us
    pallas_call x8, Pallas kernels, join(): pl.pallas_call(functools.partial(join_kernel, len(operands), keys_at, raw...  13.2 us
    ppermute x8, waiting for transfers between devices, local(): send = lambda array, route: lax.ppermute(array, AXES, route)  11.8 us
    add x1, other arithmetic, local(): first = jnp.pad(payload, ((0, KEY_ROWS), (0, 0))) + key_rows  1.31 us
  transfers between devices with their start and end apart: 8, of which 6 were waited for; matrix products, arithmetic and copies ran while one was open for 2% of the time, Pallas kernels for 20%

profile of v5, /device:TPU:1, one launch (start us, length us, event | category | flops | bytes accessed | tf_op | source)
XLA Modules:
  0.0 64.5 jit_solution(842236995572647226)
XLA Ops:
  0.0 14.4 %collective-permute-start.1 = (s32[16,128]{1,0:T(8,128)}, s32[16,128]{1,0:T(8,128)S(1)}, u32[]{:S(2)}, u32[]{:S(2)}) collective-permute-start(s32[16,128]{1,0:T(8,128)} %bitcast.2), channel_id=1, source_target_pairs={{504,0},{9,1},{506,2},{11,3},{12,4},{509,5},{14,6},{511,7},{0,8},{... | collective-permute-start | bytes 24584 | tf_op jit(solution)/shard_map/ppermute | solution.py:138
  14.4 1.3 %convert_add_fusion.refs_1_ = f32[2064,128]{1,0:T(8,128)S(1)} fusion(s32[16,128]{1,0:T(8,128)} %bitcast.7, f32[2048,128]{1,0:T(8,128)} %param.5), kind=kLoop, calls=%fused_computation.1 | loop fusion | flops 528384 | bytes 2113536 | tf_op jit(solution)/shard_map/add | solution.py:147
  15.7 1.9 %collective-permute-start = (f32[2064,128]{1,0:T(8,128)S(1)}, f32[2064,128]{1,0:T(8,128)S(1)}, u32[]{:S(2)}, u32[]{:S(2)}) collective-permute-start(f32[2064,128]{1,0:T(8,128)S(1)} %convert_add_fusion.refs_1_), channel_id=1, source_target_pairs={{0,4},{1,7},{2,6},{3,5},{4,2},{5,1},{6,0},{7,3},{8,12},{9,15},{10,... | collective-permute-start | bytes 3170312 | tf_op jit(solution)/shard_map/ppermute | solution.py:138
  17.6 0.0 collective-permute-done.1
  17.7 0.0 copy-start
  17.7 0.1 pad_maximum_fusion.refs_0_
  17.8 4.3 %collective-permute-start.2 = (f32[2080,128]{1,0:T(8,128)S(1)}, f32[2080,128]{1,0:T(8,128)S(1)}, u32[]{:S(2)}, u32[]{:S(2)}) collective-permute-start(f32[2080,128]{1,0:T(8,128)S(1)} %pad_maximum_fusion.refs_0_), channel_id=1, source_target_pairs={{0,1},{1,0},{2,3},{3,2},{4,5},{5,4},{6,7},{7,6},{8,9},{9,8},{10,11... | collective-permute-start | bytes 3194888 | tf_op jit(solution)/shard_map/ppermute | solution.py:138
  22.1 0.0 copy-done
  22.1 1.4 %home_own.1 = (f32[1024,128]{1,0:T(8,128)S(1)}, bf16[2048,256]{1,0:T(8,128)(2,1)S(1)}) custom-call(s32[16,128]{1,0:T(8,128)S(1)} %bitcast.3, f32[2064,128]{1,0:T(8,128)S(1)} %convert_add_fusion.refs_1_), custom_call_target="tpu_custom_call" | custom-call | flops 21073741824 | bytes 1572864 | tf_op jit(solution)/shard_map/home_own/pallas_call | solution.py:119
  23.6 0.8 %collective-permute-done.2.refs_1_ = f32[2080,128]{1,0:T(8,128)S(1)} collective-permute-done((f32[2080,128]{1,0:T(8,128)S(1)}, f32[2080,128]{1,0:T(8,128)S(1)}, u32[]{:S(2)}, u32[]{:S(2)}) %collective-permute-start.2) | collective-permute-done | bytes 1064992 | tf_op jit(solution)/shard_map/ppermute | solution.py:138
  24.4 2.6 %light.1 = (f32[1024,128]{1,0:T(8,128)S(1)}, bf16[2048,256]{1,0:T(8,128)(2,1)S(1)}) custom-call(f32[2080,128]{1,0:T(8,128)S(1)} %pad_maximum_fusion.refs_0_, f32[2080,128]{1,0:T(8,128)S(1)} %collective-permute-done.2.refs_1_, bf16[2048,256]{1,0:T(8,128)(2,1)S(1)} %get-tuple-element.25.refs_2_), custom_call_target="tpu_custom_call" | custom-call | flops 2147483648 | bytes 2621440 | tf_op jit(solution)/shard_map/light/pallas_call | solution.py:119
  27.0 1.3 %home_theirs.1.refs_5_ = f32[1024,128]{1,0:T(8,128)S(1)} custom-call(s32[16,128]{1,0:T(8,128)S(1)} %bitcast.4, f32[2080,128]{1,0:T(8,128)S(1)} %collective-permute-done.2.refs_1_, bf16[2048,256]{1,0:T(8,128)(2,1)S(1)} %get-tuple-element.26.refs_3_.refs_2_, f32[1024,128]{1,0:T(8,128)S(1)} %get-tuple-element.27.refs_3_), custom_call_target="tpu_custom_call" | custom-call | flops 21073741824 | bytes 2097152 | tf_op jit(solution)/shard_map/home_theirs/pallas_call | solution.py:119
  28.3 2.4 %heavy_own.1.refs_3_ = f32[1024,128]{1,0:T(8,128)S(1)} custom-call(f32[2080,128]{1,0:T(8,128)S(1)} %pad_maximum_fusion.refs_0_, f32[2080,128]{1,0:T(8,128)S(1)} %collective-permute-done.2.refs_1_, bf16[2048,256]{1,0:T(8,128)(2,1)S(1)} %get-tuple-element.25.refs_2_, bf16[2048,256]{1,0:T(8,128)(2,1)S(1)} %get-tuple-element.26.refs_3_.refs_2_), custom_call_target="tpu_custom_call" | custom-call | flops 2147483648 | bytes 2621440 | tf_op jit(solution)/shard_map/heavy_own/pallas_call | solution.py:119
  30.7 1.0 %collective-permute-done.refs_2_.refs_1_ = f32[2064,128]{1,0:T(8,128)S(1)} collective-permute-done((f32[2064,128]{1,0:T(8,128)S(1)}, f32[2064,128]{1,0:T(8,128)S(1)}, u32[]{:S(2)}, u32[]{:S(2)}) %collective-permute-start) | collective-permute-done | bytes 1056800 | tf_op jit(solution)/shard_map/ppermute | solution.py:138
  31.6 2.2 %collective-permute-start.4 = (f32[1024,128]{1,0:T(8,128)S(1)}, f32[1024,128]{1,0:T(8,128)S(1)}, u32[]{:S(2)}, u32[]{:S(2)}) collective-permute-start(f32[1024,128]{1,0:T(8,128)S(1)} %get-tuple-element.36), channel_id=1, source_target_pairs={{0,504},{1,505},{2,506},{3,507},{4,12},{5,13},{6,14},{7,15},{8,0},... | collective-permute-start | bytes 1572872 | tf_op jit(solution)/shard_map/ppermute | solution.py:138
  33.8 4.7 %collective-permute-start.3 = (f32[2064,128]{1,0:T(8,128)S(1)}, f32[2064,128]{1,0:T(8,128)S(1)}, u32[]{:S(2)}, u32[]{:S(2)}) collective-permute-start(f32[2064,128]{1,0:T(8,128)S(1)} %collective-permute-done.refs_2_.refs_1_), channel_id=1, source_target_pairs={{0,1},{1,0},{2,3},{3,2},{4,5},{5,4},{6,7},{7,6},{8,9},{9,8},{10,11... | collective-permute-start | bytes 3170312 | tf_op jit(solution)/shard_map/ppermute | solution.py:138
  38.6 1.4 %heavy_beside.1 = (f32[1024,128]{1,0:T(8,128)S(1)}, bf16[2048,256]{1,0:T(8,128)(2,1)S(1)}) custom-call(f32[2080,128]{1,0:T(8,128)S(1)} %pad_maximum_fusion.refs_0_, f32[2080,128]{1,0:T(8,128)S(1)} %collective-permute-done.2.refs_1_, f32[2064,128]{1,0:T(8,128)S(1)} %collective-permute-done.refs_2_.refs_1_, f32[1024,128]{1,0:T(8,128)S(1)} %heavy_own.1.refs_3_), custom_call_target="tpu_custom_call" | custom-call | flops 21073741824 | bytes 2097152 | tf_op jit(solution)/shard_map/heavy_beside/pallas_call | solution.py:119
  40.0 0.8 %collective-permute-done.3.refs_2_ = f32[2064,128]{1,0:T(8,128)S(1)} collective-permute-done((f32[2064,128]{1,0:T(8,128)S(1)}, f32[2064,128]{1,0:T(8,128)S(1)}, u32[]{:S(2)}, u32[]{:S(2)}) %collective-permute-start.3) | collective-permute-done | bytes 1056800 | tf_op jit(solution)/shard_map/ppermute | solution.py:138
  40.8 1.5 %heavy.1 = (f32[512,128]{1,0:T(8,128)S(1)}, f32[512,128]{1,0:T(8,128)S(1)}, bf16[2048,256]{1,0:T(8,128)(2,1)S(1)}) custom-call(f32[2080,128]{1,0:T(8,128)S(1)} %pad_maximum_fusion.refs_0_, f32[2080,128]{1,0:T(8,128)S(1)} %collective-permute-done.2.refs_1_, f32[2064,128]{1,0:T(8,128)S(1)} %collective-permute-done.3.refs_2_, ...), custom_call_target="tpu_custom_call" | custom-call | flops 1073741824 | bytes 2097152 | tf_op jit(solution)/shard_map/heavy/pallas_call | solution.py:119
  42.3 3.5 %collective-permute-start.5 = (f32[512,128]{1,0:T(8,128)S(1)}, f32[512,128]{1,0:T(8,128)S(1)}, u32[]{:S(2)}, u32[]{:S(2)}) collective-permute-start(f32[512,128]{1,0:T(8,128)S(1)} %get-tuple-element.37), channel_id=1, source_target_pairs={{0,10},{1,11},{2,8},{3,9},{4,510},{5,511},{6,508},{7,509},{8,18},{... | collective-permute-start | bytes 786440 | tf_op jit(solution)/shard_map/ppermute | solution.py:138
  45.8 1.9 %collective-permute-start.6 = (f32[512,128]{1,0:T(8,128)S(1)}, f32[512,128]{1,0:T(8,128)S(1)}, u32[]{:S(2)}, u32[]{:S(2)}) collective-permute-start(f32[512,128]{1,0:T(8,128)S(1)} %get-tuple-element.38), channel_id=1, source_target_pairs={{0,8},{1,9},{2,10},{3,11},{4,508},{5,509},{6,510},{7,511},{8,16},{... | collective-permute-start | bytes 786440 | tf_op jit(solution)/shard_map/ppermute | solution.py:138
  47.8 0.0 collective-permute-done.4.refs_6_
  47.8 1.3 %home_other.1 = f32[512,128]{1,0:T(8,128)S(1)} custom-call(s32[16,128]{1,0:T(8,128)S(1)} %bitcast.5, f32[2064,128]{1,0:T(8,128)S(1)} %collective-permute-done.refs_2_.refs_1_, f32[2064,128]{1,0:T(8,128)S(1)} %collective-permute-done.3.refs_2_, bf16[2048,256]{1,0:T(8,128)(2,1)S(1)} %get-tuple-element.32.refs_3_, ...), custom_call_target="tpu_custom_call" | custom-call | flops 1073741824 | bytes 2883584 | tf_op jit(solution)/shard_map/home_other/pallas_call | solution.py:119
  49.1 4.2 %collective-permute-start.7 = (f32[512,128]{1,0:T(8,128)S(1)}, f32[512,128]{1,0:T(8,128)S(1)}, u32[]{:S(2)}, u32[]{:S(2)}) collective-permute-start(f32[512,128]{1,0:T(8,128)S(1)} %home_other.1), channel_id=1, source_target_pairs={{0,2},{1,3},{2,0},{3,1},{4,6},{5,7},{6,4},{7,5},{8,10},{9,11},{10,... | collective-permute-start | bytes 786440 | tf_op jit(solution)/shard_map/ppermute | solution.py:138
  53.3 4.2 %collective-permute-done.5.refs_7_ = f32[512,128]{1,0:T(8,128)S(1)} collective-permute-done((f32[512,128]{1,0:T(8,128)S(1)}, f32[512,128]{1,0:T(8,128)S(1)}, u32[]{:S(2)}, u32[]{:S(2)}) %collective-permute-start.5) | collective-permute-done | bytes 262176 | tf_op jit(solution)/shard_map/ppermute | solution.py:138
  57.4 4.4 %collective-permute-done.6.refs_8_ = f32[512,128]{1,0:T(8,128)S(1)} collective-permute-done((f32[512,128]{1,0:T(8,128)S(1)}, f32[512,128]{1,0:T(8,128)S(1)}, u32[]{:S(2)}, u32[]{:S(2)}) %collective-permute-start.6) | collective-permute-done | bytes 262176 | tf_op jit(solution)/shard_map/ppermute | solution.py:138
  61.8 1.3 %home_same.1 = f32[512,128]{1,0:T(8,128)S(1)} custom-call(s32[16,128]{1,0:T(8,128)S(1)} %bitcast.6, f32[2064,128]{1,0:T(8,128)S(1)} %collective-permute-done.refs_2_.refs_1_, f32[2064,128]{1,0:T(8,128)S(1)} %collective-permute-done.3.refs_2_, bf16[2048,256]{1,0:T(8,128)(2,1)S(1)} %get-tuple-element.32.refs_3_, ...), custom_call_target="tpu_custom_call" | custom-call | flops 1073741824 | bytes 3407872 | tf_op jit(solution)/shard_map/home_same/pallas_call | solution.py:119
  63.1 0.6 collective-permute-done.7
  63.8 0.7 %add.11 = f32[512,128]{1,0:T(8,128)} add(f32[512,128]{1,0:T(8,128)S(1)} %home_same.1, f32[512,128]{1,0:T(8,128)S(1)} %collective-permute-done.7) | non-fusion elementwise | flops 65536 | bytes 786432 | tf_op jit(solution)/shard_map/add | solution.py:180
  (1 shorter events, 0.0 us)
Async XLA Ops:
  0.0 17.6 %collective-permute-start.1 = (s32[16,128]{1,0:T(8,128)}, s32[16,128]{1,0:T(8,128)S(1)}, u32[]{:S(2)}, u32[]{:S(2)}) collective-permute-start(s32[16,128]{1,0:T(8,128)} %bitcast.2), channel_id=1, source_target_pairs={{504,0},{9,1},{506,2},{11,3},{12,4},{509,5},{14,6},{511,7},{0,8},{... | collective-permute-start | bytes 24584 | tf_op jit(solution)/shard_map/ppermute | solution.py:138
  15.7 15.9 %collective-permute-start = (f32[2064,128]{1,0:T(8,128)S(1)}, f32[2064,128]{1,0:T(8,128)S(1)}, u32[]{:S(2)}, u32[]{:S(2)}) collective-permute-start(f32[2064,128]{1,0:T(8,128)S(1)} %convert_add_fusion.refs_1_), channel_id=1, source_target_pairs={{0,4},{1,7},{2,6},{3,5},{4,2},{5,1},{6,0},{7,3},{8,12},{9,15},{10,... | collective-permute-start | bytes 3170312 | tf_op jit(solution)/shard_map/ppermute | solution.py:138
  17.7 4.4 %copy-start = (s32[2048]{0:T(1024)S(1)}, s32[2048]{0:T(1024)}, u32[]{:S(2)}) copy-start(s32[2048]{0:T(1024)} %param.3) | copy-start | bytes 24580
  17.8 6.6 %collective-permute-start.2 = (f32[2080,128]{1,0:T(8,128)S(1)}, f32[2080,128]{1,0:T(8,128)S(1)}, u32[]{:S(2)}, u32[]{:S(2)}) collective-permute-start(f32[2080,128]{1,0:T(8,128)S(1)} %pad_maximum_fusion.refs_0_), channel_id=1, source_target_pairs={{0,1},{1,0},{2,3},{3,2},{4,5},{5,4},{6,7},{7,6},{8,9},{9,8},{10,11... | collective-permute-start | bytes 3194888 | tf_op jit(solution)/shard_map/ppermute | solution.py:138
  31.6 16.1 %collective-permute-start.4 = (f32[1024,128]{1,0:T(8,128)S(1)}, f32[1024,128]{1,0:T(8,128)S(1)}, u32[]{:S(2)}, u32[]{:S(2)}) collective-permute-start(f32[1024,128]{1,0:T(8,128)S(1)} %get-tuple-element.36), channel_id=1, source_target_pairs={{0,504},{1,505},{2,506},{3,507},{4,12},{5,13},{6,14},{7,15},{8,0},... | collective-permute-start | bytes 1572872 | tf_op jit(solution)/shard_map/ppermute | solution.py:138
  33.8 7.0 %collective-permute-start.3 = (f32[2064,128]{1,0:T(8,128)S(1)}, f32[2064,128]{1,0:T(8,128)S(1)}, u32[]{:S(2)}, u32[]{:S(2)}) collective-permute-start(f32[2064,128]{1,0:T(8,128)S(1)} %collective-permute-done.refs_2_.refs_1_), channel_id=1, source_target_pairs={{0,1},{1,0},{2,3},{3,2},{4,5},{5,4},{6,7},{7,6},{8,9},{9,8},{10,11... | collective-permute-start | bytes 3170312 | tf_op jit(solution)/shard_map/ppermute | solution.py:138
  42.3 15.1 %collective-permute-start.5 = (f32[512,128]{1,0:T(8,128)S(1)}, f32[512,128]{1,0:T(8,128)S(1)}, u32[]{:S(2)}, u32[]{:S(2)}) collective-permute-start(f32[512,128]{1,0:T(8,128)S(1)} %get-tuple-element.37), channel_id=1, source_target_pairs={{0,10},{1,11},{2,8},{3,9},{4,510},{5,511},{6,508},{7,509},{8,18},{... | collective-permute-start | bytes 786440 | tf_op jit(solution)/shard_map/ppermute | solution.py:138
  45.8 16.0 %collective-permute-start.6 = (f32[512,128]{1,0:T(8,128)S(1)}, f32[512,128]{1,0:T(8,128)S(1)}, u32[]{:S(2)}, u32[]{:S(2)}) collective-permute-start(f32[512,128]{1,0:T(8,128)S(1)} %get-tuple-element.38), channel_id=1, source_target_pairs={{0,8},{1,9},{2,10},{3,11},{4,508},{5,509},{6,510},{7,511},{8,16},{... | collective-permute-start | bytes 786440 | tf_op jit(solution)/shard_map/ppermute | solution.py:138
  49.1 14.7 %collective-permute-start.7 = (f32[512,128]{1,0:T(8,128)S(1)}, f32[512,128]{1,0:T(8,128)S(1)}, u32[]{:S(2)}, u32[]{:S(2)}) collective-permute-start(f32[512,128]{1,0:T(8,128)S(1)} %home_other.1), channel_id=1, source_target_pairs={{0,2},{1,3},{2,0},{3,1},{4,6},{5,7},{6,4},{7,5},{8,10},{9,11},{10,... | collective-permute-start | bytes 786440 | tf_op jit(solution)/shard_map/ppermute | solution.py:138

commit v6 on v5

--- a/solution.py
+++ b/solution.py
@@ -139,14 +139,12 @@
     own_keys = resident_keys.reshape(KEY_ROWS, LANES)
     home_keys = [(own_keys, 0)]
 
-    def packed(above, keys):
-        return jnp.concatenate([above, keys.reshape(KEY_ROWS, LANES).astype(jnp.float32)], axis=0)
-
     fetched = send(own_keys, fetch)
     key_rows = jnp.pad(moving_keys.reshape(KEY_ROWS, LANES), ((S_DEV, 0), (0, 0))).astype(jnp.float32)
     first = jnp.pad(payload, ((0, KEY_ROWS), (0, 0))) + key_rows
     beside = send(first, near)
-    mine = packed(first, fetched)
+    fetched_rows = jnp.pad(fetched, ((S_DEV + KEY_ROWS, 0), (0, 0))).astype(jnp.float32)
+    mine = jnp.pad(first, ((0, KEY_ROWS), (0, 0))) + fetched_rows
     theirs = send(mine, swap)
     home, mine_parts = join("home_own", home_keys, [(first, None)], [], (0, 1), weight=W_HOME_OWN)
     theirs, home, mine_parts = lax.optimization_barrier((theirs, home, mine_parts))

time: 64.9 us -> 64.9 us (level)
  no operation moved by 1% of the time
where the time goes in v6:
time: 64.9 us; the launch traced here: 64.5 us
  starting transfers between devices  37.2 us (57%)
  Pallas kernels  13.2 us (20%)
  waiting for transfers between devices  11.8 us (18%)
  other arithmetic  2.12 us (3%)
    ppermute x8, starting transfers between devices, local(): send = lambda array, route: lax.ppermute(array, AXES, route)  37.2 us
    pallas_call x8, Pallas kernels, join(): pl.pallas_call(functools.partial(join_kernel, len(operands), keys_at, raw...  13.2 us
    ppermute x8, waiting for transfers between devices, local(): send = lambda array, route: lax.ppermute(array, AXES, route)  11.8 us
    add x1, other arithmetic, local(): first = jnp.pad(payload, ((0, KEY_ROWS), (0, 0))) + key_rows  1.31 us
  transfers between devices with their start and end apart: 8, of which 6 were waited for; matrix products, arithmetic and copies ran while one was open for 2% of the time, Pallas kernels for 20%

profile of v6, /device:TPU:1, one launch (start us, length us, event | category | flops | bytes accessed | tf_op | source)
XLA Modules:
  0.0 64.5 jit_solution(6469258595819508118)
XLA Ops:
  0.0 14.4 %collective-permute-start.1 = (s32[16,128]{1,0:T(8,128)}, s32[16,128]{1,0:T(8,128)S(1)}, u32[]{:S(2)}, u32[]{:S(2)}) collective-permute-start(s32[16,128]{1,0:T(8,128)} %bitcast.2), channel_id=1, source_target_pairs={{504,0},{9,1},{506,2},{11,3},{12,4},{509,5},{14,6},{511,7},{0,8},{... | collective-permute-start | bytes 24584 | tf_op jit(solution)/shard_map/ppermute | solution.py:138
  14.4 1.3 %convert_add_fusion.1.refs_1_ = f32[2064,128]{1,0:T(8,128)S(1)} fusion(s32[16,128]{1,0:T(8,128)} %bitcast.7, f32[2048,128]{1,0:T(8,128)} %param.5), kind=kLoop, calls=%fused_computation.1 | loop fusion | flops 528384 | bytes 2113536 | tf_op jit(solution)/shard_map/add | solution.py:144
  15.7 0.0 copy-start
  15.7 1.9 %collective-permute-start = (f32[2064,128]{1,0:T(8,128)S(1)}, f32[2064,128]{1,0:T(8,128)S(1)}, u32[]{:S(2)}, u32[]{:S(2)}) collective-permute-start(f32[2064,128]{1,0:T(8,128)S(1)} %convert_add_fusion.1.refs_1_), channel_id=1, source_target_pairs={{0,4},{1,7},{2,6},{3,5},{4,2},{5,1},{6,0},{7,3},{8,12},{9,15},{10,... | collective-permute-start | bytes 3170312 | tf_op jit(solution)/shard_map/ppermute | solution.py:138
  17.7 0.0 collective-permute-done.1
  17.7 0.1 convert_add_fusion.refs_0_
  17.7 4.3 %collective-permute-start.2 = (f32[2080,128]{1,0:T(8,128)S(1)}, f32[2080,128]{1,0:T(8,128)S(1)}, u32[]{:S(2)}, u32[]{:S(2)}) collective-permute-start(f32[2080,128]{1,0:T(8,128)S(1)} %convert_add_fusion.refs_0_), channel_id=1, source_target_pairs={{0,1},{1,0},{2,3},{3,2},{4,5},{5,4},{6,7},{7,6},{8,9},{9,8},{10,11... | collective-permute-start | bytes 3194888 | tf_op jit(solution)/shard_map/ppermute | solution.py:138
  22.1 0.0 copy-done
  22.1 1.4 %home_own.1 = (f32[1024,128]{1,0:T(8,128)S(1)}, bf16[2048,256]{1,0:T(8,128)(2,1)S(1)}) custom-call(s32[16,128]{1,0:T(8,128)S(1)} %bitcast.3, f32[2064,128]{1,0:T(8,128)S(1)} %convert_add_fusion.1.refs_1_), custom_call_target="tpu_custom_call" | custom-call | flops 21073741824 | bytes 1572864 | tf_op jit(solution)/shard_map/home_own/pallas_call | solution.py:119
  23.5 0.8 %collective-permute-done.2.refs_1_ = f32[2080,128]{1,0:T(8,128)S(1)} collective-permute-done((f32[2080,128]{1,0:T(8,128)S(1)}, f32[2080,128]{1,0:T(8,128)S(1)}, u32[]{:S(2)}, u32[]{:S(2)}) %collective-permute-start.2) | collective-permute-done | bytes 1064992 | tf_op jit(solution)/shard_map/ppermute | solution.py:138
  24.4 2.6 %light.1 = (f32[1024,128]{1,0:T(8,128)S(1)}, bf16[2048,256]{1,0:T(8,128)(2,1)S(1)}) custom-call(f32[2080,128]{1,0:T(8,128)S(1)} %convert_add_fusion.refs_0_, f32[2080,128]{1,0:T(8,128)S(1)} %collective-permute-done.2.refs_1_, bf16[2048,256]{1,0:T(8,128)(2,1)S(1)} %get-tuple-element.25.refs_2_), custom_call_target="tpu_custom_call" | custom-call | flops 2147483648 | bytes 2621440 | tf_op jit(solution)/shard_map/light/pallas_call | solution.py:119
  27.0 1.3 %home_theirs.1.refs_5_ = f32[1024,128]{1,0:T(8,128)S(1)} custom-call(s32[16,128]{1,0:T(8,128)S(1)} %bitcast.4, f32[2080,128]{1,0:T(8,128)S(1)} %collective-permute-done.2.refs_1_, bf16[2048,256]{1,0:T(8,128)(2,1)S(1)} %get-tuple-element.26.refs_3_.refs_2_, f32[1024,128]{1,0:T(8,128)S(1)} %get-tuple-element.27.refs_3_), custom_call_target="tpu_custom_call" | custom-call | flops 21073741824 | bytes 2097152 | tf_op jit(solution)/shard_map/home_theirs/pallas_call | solution.py:119
  28.3 2.4 %heavy_own.1.refs_3_ = f32[1024,128]{1,0:T(8,128)S(1)} custom-call(f32[2080,128]{1,0:T(8,128)S(1)} %convert_add_fusion.refs_0_, f32[2080,128]{1,0:T(8,128)S(1)} %collective-permute-done.2.refs_1_, bf16[2048,256]{1,0:T(8,128)(2,1)S(1)} %get-tuple-element.25.refs_2_, bf16[2048,256]{1,0:T(8,128)(2,1)S(1)} %get-tuple-element.26.refs_3_.refs_2_), custom_call_target="tpu_custom_call" | custom-call | flops 2147483648 | bytes 2621440 | tf_op jit(solution)/shard_map/heavy_own/pallas_call | solution.py:119
  30.7 1.0 %collective-permute-done.refs_2_.refs_1_ = f32[2064,128]{1,0:T(8,128)S(1)} collective-permute-done((f32[2064,128]{1,0:T(8,128)S(1)}, f32[2064,128]{1,0:T(8,128)S(1)}, u32[]{:S(2)}, u32[]{:S(2)}) %collective-permute-start) | collective-permute-done | bytes 1056800 | tf_op jit(solution)/shard_map/ppermute | solution.py:138
  31.7 2.2 %collective-permute-start.4 = (f32[1024,128]{1,0:T(8,128)S(1)}, f32[1024,128]{1,0:T(8,128)S(1)}, u32[]{:S(2)}, u32[]{:S(2)}) collective-permute-start(f32[1024,128]{1,0:T(8,128)S(1)} %get-tuple-element.36), channel_id=1, source_target_pairs={{0,504},{1,505},{2,506},{3,507},{4,12},{5,13},{6,14},{7,15},{8,0},... | collective-permute-start | bytes 1572872 | tf_op jit(solution)/shard_map/ppermute | solution.py:138
  33.9 4.7 %collective-permute-start.3 = (f32[2064,128]{1,0:T(8,128)S(1)}, f32[2064,128]{1,0:T(8,128)S(1)}, u32[]{:S(2)}, u32[]{:S(2)}) collective-permute-start(f32[2064,128]{1,0:T(8,128)S(1)} %collective-permute-done.refs_2_.refs_1_), channel_id=1, source_target_pairs={{0,1},{1,0},{2,3},{3,2},{4,5},{5,4},{6,7},{7,6},{8,9},{9,8},{10,11... | collective-permute-start | bytes 3170312 | tf_op jit(solution)/shard_map/ppermute | solution.py:138
  38.6 1.4 %heavy_beside.1 = (f32[1024,128]{1,0:T(8,128)S(1)}, bf16[2048,256]{1,0:T(8,128)(2,1)S(1)}) custom-call(f32[2080,128]{1,0:T(8,128)S(1)} %convert_add_fusion.refs_0_, f32[2080,128]{1,0:T(8,128)S(1)} %collective-permute-done.2.refs_1_, f32[2064,128]{1,0:T(8,128)S(1)} %collective-permute-done.refs_2_.refs_1_, f32[1024,128]{1,0:T(8,128)S(1)} %heavy_own.1.refs_3_), custom_call_target="tpu_custom_call" | custom-call | flops 21073741824 | bytes 2097152 | tf_op jit(solution)/shard_map/heavy_beside/pallas_call | solution.py:119
  40.0 0.8 %collective-permute-done.3.refs_2_ = f32[2064,128]{1,0:T(8,128)S(1)} collective-permute-done((f32[2064,128]{1,0:T(8,128)S(1)}, f32[2064,128]{1,0:T(8,128)S(1)}, u32[]{:S(2)}, u32[]{:S(2)}) %collective-permute-start.3) | collective-permute-done | bytes 1056800 | tf_op jit(solution)/shard_map/ppermute | solution.py:138
  40.9 1.5 %heavy.1 = (f32[512,128]{1,0:T(8,128)S(1)}, f32[512,128]{1,0:T(8,128)S(1)}, bf16[2048,256]{1,0:T(8,128)(2,1)S(1)}) custom-call(f32[2080,128]{1,0:T(8,128)S(1)} %convert_add_fusion.refs_0_, f32[2080,128]{1,0:T(8,128)S(1)} %collective-permute-done.2.refs_1_, f32[2064,128]{1,0:T(8,128)S(1)} %collective-permute-done.3.refs_2_, ...), custom_call_target="tpu_custom_call" | custom-call | flops 1073741824 | bytes 2097152 | tf_op jit(solution)/shard_map/heavy/pallas_call | solution.py:119
  42.3 3.5 %collective-permute-start.5 = (f32[512,128]{1,0:T(8,128)S(1)}, f32[512,128]{1,0:T(8,128)S(1)}, u32[]{:S(2)}, u32[]{:S(2)}) collective-permute-start(f32[512,128]{1,0:T(8,128)S(1)} %get-tuple-element.37), channel_id=1, source_target_pairs={{0,10},{1,11},{2,8},{3,9},{4,510},{5,511},{6,508},{7,509},{8,18},{... | collective-permute-start | bytes 786440 | tf_op jit(solution)/shard_map/ppermute | solution.py:138
  45.9 1.9 %collective-permute-start.6 = (f32[512,128]{1,0:T(8,128)S(1)}, f32[512,128]{1,0:T(8,128)S(1)}, u32[]{:S(2)}, u32[]{:S(2)}) collective-permute-start(f32[512,128]{1,0:T(8,128)S(1)} %get-tuple-element.38), channel_id=1, source_target_pairs={{0,8},{1,9},{2,10},{3,11},{4,508},{5,509},{6,510},{7,511},{8,16},{... | collective-permute-start | bytes 786440 | tf_op jit(solution)/shard_map/ppermute | solution.py:138
  47.8 0.0 collective-permute-done.4.refs_6_
  47.8 1.3 %home_other.1 = f32[512,128]{1,0:T(8,128)S(1)} custom-call(s32[16,128]{1,0:T(8,128)S(1)} %bitcast.5, f32[2064,128]{1,0:T(8,128)S(1)} %collective-permute-done.refs_2_.refs_1_, f32[2064,128]{1,0:T(8,128)S(1)} %collective-permute-done.3.refs_2_, bf16[2048,256]{1,0:T(8,128)(2,1)S(1)} %get-tuple-element.32.refs_3_, ...), custom_call_target="tpu_custom_call" | custom-call | flops 1073741824 | bytes 2883584 | tf_op jit(solution)/shard_map/home_other/pallas_call | solution.py:119
  49.1 4.2 %collective-permute-start.7 = (f32[512,128]{1,0:T(8,128)S(1)}, f32[512,128]{1,0:T(8,128)S(1)}, u32[]{:S(2)}, u32[]{:S(2)}) collective-permute-start(f32[512,128]{1,0:T(8,128)S(1)} %home_other.1), channel_id=1, source_target_pairs={{0,2},{1,3},{2,0},{3,1},{4,6},{5,7},{6,4},{7,5},{8,10},{9,11},{10,... | collective-permute-start | bytes 786440 | tf_op jit(solution)/shard_map/ppermute | solution.py:138
  53.3 4.2 %collective-permute-done.5.refs_7_ = f32[512,128]{1,0:T(8,128)S(1)} collective-permute-done((f32[512,128]{1,0:T(8,128)S(1)}, f32[512,128]{1,0:T(8,128)S(1)}, u32[]{:S(2)}, u32[]{:S(2)}) %collective-permute-start.5) | collective-permute-done | bytes 262176 | tf_op jit(solution)/shard_map/ppermute | solution.py:138
  57.4 4.4 %collective-permute-done.6.refs_8_ = f32[512,128]{1,0:T(8,128)S(1)} collective-permute-done((f32[512,128]{1,0:T(8,128)S(1)}, f32[512,128]{1,0:T(8,128)S(1)}, u32[]{:S(2)}, u32[]{:S(2)}) %collective-permute-start.6) | collective-permute-done | bytes 262176 | tf_op jit(solution)/shard_map/ppermute | solution.py:138
  61.8 1.3 %home_same.1 = f32[512,128]{1,0:T(8,128)S(1)} custom-call(s32[16,128]{1,0:T(8,128)S(1)} %bitcast.6, f32[2064,128]{1,0:T(8,128)S(1)} %collective-permute-done.refs_2_.refs_1_, f32[2064,128]{1,0:T(8,128)S(1)} %collective-permute-done.3.refs_2_, bf16[2048,256]{1,0:T(8,128)(2,1)S(1)} %get-tuple-element.32.refs_3_, ...), custom_call_target="tpu_custom_call" | custom-call | flops 1073741824 | bytes 3407872 | tf_op jit(solution)/shard_map/home_same/pallas_call | solution.py:119
  63.1 0.6 collective-permute-done.7
  63.8 0.7 %add.19 = f32[512,128]{1,0:T(8,128)} add(f32[512,128]{1,0:T(8,128)S(1)} %home_same.1, f32[512,128]{1,0:T(8,128)S(1)} %collective-permute-done.7) | non-fusion elementwise | flops 65536 | bytes 786432 | tf_op jit(solution)/shard_map/add | solution.py:178
Async XLA Ops:
  0.0 17.7 %collective-permute-start.1 = (s32[16,128]{1,0:T(8,128)}, s32[16,128]{1,0:T(8,128)S(1)}, u32[]{:S(2)}, u32[]{:S(2)}) collective-permute-start(s32[16,128]{1,0:T(8,128)} %bitcast.2), channel_id=1, source_target_pairs={{504,0},{9,1},{506,2},{11,3},{12,4},{509,5},{14,6},{511,7},{0,8},{... | collective-permute-start | bytes 24584 | tf_op jit(solution)/shard_map/ppermute | solution.py:138
  15.7 6.4 %copy-start = (s32[2048]{0:T(1024)S(1)}, s32[2048]{0:T(1024)}, u32[]{:S(2)}) copy-start(s32[2048]{0:T(1024)} %param.3) | copy-start | bytes 24580
  15.7 15.9 %collective-permute-start = (f32[2064,128]{1,0:T(8,128)S(1)}, f32[2064,128]{1,0:T(8,128)S(1)}, u32[]{:S(2)}, u32[]{:S(2)}) collective-permute-start(f32[2064,128]{1,0:T(8,128)S(1)} %convert_add_fusion.1.refs_1_), channel_id=1, source_target_pairs={{0,4},{1,7},{2,6},{3,5},{4,2},{5,1},{6,0},{7,3},{8,12},{9,15},{10,... | collective-permute-start | bytes 3170312 | tf_op jit(solution)/shard_map/ppermute | solution.py:138
  17.7 6.6 %collective-permute-start.2 = (f32[2080,128]{1,0:T(8,128)S(1)}, f32[2080,128]{1,0:T(8,128)S(1)}, u32[]{:S(2)}, u32[]{:S(2)}) collective-permute-start(f32[2080,128]{1,0:T(8,128)S(1)} %convert_add_fusion.refs_0_), channel_id=1, source_target_pairs={{0,1},{1,0},{2,3},{3,2},{4,5},{5,4},{6,7},{7,6},{8,9},{9,8},{10,11... | collective-permute-start | bytes 3194888 | tf_op jit(solution)/shard_map/ppermute | solution.py:138
  31.7 16.1 %collective-permute-start.4 = (f32[1024,128]{1,0:T(8,128)S(1)}, f32[1024,128]{1,0:T(8,128)S(1)}, u32[]{:S(2)}, u32[]{:S(2)}) collective-permute-start(f32[1024,128]{1,0:T(8,128)S(1)} %get-tuple-element.36), channel_id=1, source_target_pairs={{0,504},{1,505},{2,506},{3,507},{4,12},{5,13},{6,14},{7,15},{8,0},... | collective-permute-start | bytes 1572872 | tf_op jit(solution)/shard_map/ppermute | solution.py:138
  33.9 7.0 %collective-permute-start.3 = (f32[2064,128]{1,0:T(8,128)S(1)}, f32[2064,128]{1,0:T(8,128)S(1)}, u32[]{:S(2)}, u32[]{:S(2)}) collective-permute-start(f32[2064,128]{1,0:T(8,128)S(1)} %collective-permute-done.refs_2_.refs_1_), channel_id=1, source_target_pairs={{0,1},{1,0},{2,3},{3,2},{4,5},{5,4},{6,7},{7,6},{8,9},{9,8},{10,11... | collective-permute-start | bytes 3170312 | tf_op jit(solution)/shard_map/ppermute | solution.py:138
  42.3 15.1 %collective-permute-start.5 = (f32[512,128]{1,0:T(8,128)S(1)}, f32[512,128]{1,0:T(8,128)S(1)}, u32[]{:S(2)}, u32[]{:S(2)}) collective-permute-start(f32[512,128]{1,0:T(8,128)S(1)} %get-tuple-element.37), channel_id=1, source_target_pairs={{0,10},{1,11},{2,8},{3,9},{4,510},{5,511},{6,508},{7,509},{8,18},{... | collective-permute-start | bytes 786440 | tf_op jit(solution)/shard_map/ppermute | solution.py:138
  45.9 16.0 %collective-permute-start.6 = (f32[512,128]{1,0:T(8,128)S(1)}, f32[512,128]{1,0:T(8,128)S(1)}, u32[]{:S(2)}, u32[]{:S(2)}) collective-permute-start(f32[512,128]{1,0:T(8,128)S(1)} %get-tuple-element.38), channel_id=1, source_target_pairs={{0,8},{1,9},{2,10},{3,11},{4,508},{5,509},{6,510},{7,511},{8,16},{... | collective-permute-start | bytes 786440 | tf_op jit(solution)/shard_map/ppermute | solution.py:138
  49.1 14.7 %collective-permute-start.7 = (f32[512,128]{1,0:T(8,128)S(1)}, f32[512,128]{1,0:T(8,128)S(1)}, u32[]{:S(2)}, u32[]{:S(2)}) collective-permute-start(f32[512,128]{1,0:T(8,128)S(1)} %home_other.1), channel_id=1, source_target_pairs={{0,2},{1,3},{2,0},{3,1},{4,6},{5,7},{6,4},{7,5},{8,10},{9,11},{10,... | collective-permute-start | bytes 786440 | tf_op jit(solution)/shard_map/ppermute | solution.py:138
